TPU v7x, 512 devices: a whole 4x4x16 slice. The times are simulated.
512 devices in a mesh: dp: 32 (over z, core), expert: 16 (over x, y).
Axes of the slice: x: 4, y: 4, z: 16, core: 2. Of those that a mesh axis runs over, the one named last changes fastest.
Arguments:
- tokens: bfloat16 [65536, 2560], P(('dp', 'expert')), may hold values from -24 to 24
- out_grad: bfloat16 [65536, 2560], P(('dp', 'expert')), may hold values from -0.29882812 to 0.29882812
- gate_up: bfloat16 [65536, 1, 1536], P(('dp', 'expert')), may hold values from -8 to 8
- route_weight: bfloat16 [65536, 1], P(('dp', 'expert')), may hold values from 0.19921875 to 1
- routes: int32 [65536, 1], P(('dp', 'expert')), may hold values from 0 to 15; in each aligned block of 128 rows (0 to 127, 128 to 255, ...) at most 16 rows name the same one
- down_weight: bfloat16 [16, 768, 2560], P('expert', 'dp'), may hold values from -0.21875 to 0.21875
- master: float32 [16, 32, 126720], P('expert', 'dp'), may hold values from -0.12 to 0.12
- moment_one: float32 [16, 32, 126720], P('expert', 'dp'), may hold values from -2 to 2
- moment_two: float32 [16, 32, 126720], P('expert', 'dp'), may hold values from 0.05 to 5
- offsets: int32 [33], replicated, may hold values from 0 to 3932160, as said below
Outputs:
- new_master: float32 [16, 32, 126720], P('expert', 'dp')
- new_moment_one: float32 [16, 32, 126720], P('expert', 'dp')
- new_moment_two: float32 [16, 32, 126720], P('expert', 'dp')
- new_weight: bfloat16 [16, 2560, 1536], P('expert', 'dp')
- router_grad: float32 [65536, 1], P(('dp', 'expert'))
Inputs may be any that keep to these rules, and one draw needn't show every extreme that they name: `routes`: in each aligned block of 128 tokens (the tokens of one device) no expert is named more than 16 times, a bound that some block reaches; the 1 choices of a token differ. offsets[0] = 0, offsets[32] = 3932160; for 0 < j < 32, offsets[j] lies from j * 122880 - 3840 to j * 122880 - 2; offsets[31] = 3805440, so the last bucket holds exactly 126720 entries.
All inputs are finite; a program needn't handle non-finite values.
Results may differ from a plain program's by a relative error of at most 0.0012.
Values may be sent and summed in bfloat16 or wider, within the bound.
A program may use at most 128 MiB of HBM per device.

v0:
```python
import jax
import jax.numpy as jnp
from jax import lax
from jax.sharding import PartitionSpec as P

beta_one = 0.9
beta_two = 0.95
learn_rate = 0.001
decay_rate = 0.1
adam_eps = 1e-08
adam_step = 20.0


def shifted(block, axis, distance):
    devices = range(lax.axis_size(axis))
    route = [(i - distance, i) for i in devices if i - distance in devices]
    return lax.ppermute(block, axis, route)


def cut_window(source, from_index, window_len):
    return lax.dynamic_slice_in_dim(source, from_index, window_len, 1)


def zero_cols(row_count, col_count, kind):
    return jnp.zeros((row_count, col_count), kind)


def shards(
    tokens,
    out_grad,
    gate_up,
    route_weight,
    routes,
    down_weight,
    master,
    moment_one,
    moment_two,
    offsets,
):
    token_count, model_width = tokens.shape
    choice_count = routes.shape[1]
    hidden = gate_up.shape[2] // 2
    local_experts = master.shape[0]
    bucket_cap = master.shape[2]
    groups = lax.axis_size("expert")
    dp_count = lax.axis_size("dp")
    experts = groups * local_experts
    row_count = token_count * choice_count
    capacity = 2 * row_count // experts
    row_expert = routes.reshape(row_count)
    onehot = (row_expert[:, None] == jnp.arange(experts, dtype=jnp.int32)[None, :]).astype(
        jnp.int32
    )
    earlier = jnp.cumsum(onehot, axis=0) - onehot
    row_slot = jnp.sum(earlier * onehot, axis=1)
    target = jnp.arange(experts * capacity, dtype=jnp.int32)
    select = (
        (row_expert[None, :] == target[:, None] // capacity)
        & (row_slot[None, :] == target[:, None] % capacity)
    ).astype(jnp.bfloat16)
    row_tokens = jnp.repeat(tokens, choice_count, axis=0)
    row_grads = jnp.repeat(out_grad, choice_count, axis=0)
    payload = jnp.concatenate(
        [row_tokens, row_grads, gate_up.reshape(row_count, 2 * hidden)], axis=1
    )
    packed = jnp.dot(select, payload, preferred_element_type=jnp.float32).astype(jnp.bfloat16)
    packed = packed.reshape(experts, capacity, payload.shape[1])
    weight_sent = jnp.dot(select, route_weight, preferred_element_type=jnp.float32)
    weight_sent = weight_sent.reshape(experts, capacity).astype(jnp.bfloat16)
    arrived, arrived_weight = (
        lax.all_to_all(packed, "expert", split_axis=0, concat_axis=1, tiled=True),
        lax.all_to_all(weight_sent, "expert", split_axis=0, concat_axis=1, tiled=True),
    )
    features = arrived[:, :, :model_width]
    cotangent = arrived[:, :, model_width : 2 * model_width]
    saved_gu = arrived[:, :, 2 * model_width :]
    back_prod = jnp.einsum(
        "lrd,lkd->lrk",
        cotangent,
        lax.all_gather(down_weight, "dp", axis=1, tiled=True),
        preferred_element_type=jnp.float32,
    )
    gate_pre = saved_gu[:, :, :hidden].astype(jnp.float32)
    up_part = saved_gu[:, :, hidden:].astype(jnp.float32)
    sigmoid_gate = jax.nn.sigmoid(gate_pre)
    activation = gate_pre * sigmoid_gate * up_part
    scores = jnp.sum(activation * back_prod, axis=2)
    scaled = arrived_weight.astype(jnp.float32)[:, :, None] * back_prod
    grad_gate = scaled * up_part * sigmoid_gate * (1.0 + gate_pre * (1.0 - sigmoid_gate))
    grad_up = scaled * gate_pre * sigmoid_gate
    grad_joined = jnp.concatenate([grad_gate, grad_up], axis=2).astype(jnp.bfloat16)
    partial_sum = jnp.einsum(
        "lrd,lrj->ldj", features, grad_joined, preferred_element_type=jnp.float32
    ).astype(jnp.bfloat16)
    returned = lax.all_to_all(scores, "expert", split_axis=1, concat_axis=0, tiled=True)
    flat_scores = returned.reshape(experts * capacity)
    router_grad = jnp.take(flat_scores, row_expert * capacity + row_slot).reshape(
        token_count, choice_count
    )
    flat_size = partial_sum.shape[1] * partial_sum.shape[2]
    flat_part = partial_sum.reshape(local_experts, flat_size)
    even_size = flat_size // dp_count
    margin_size = bucket_cap - even_size
    position = lax.axis_index("dp")
    start_at = offsets[position]
    finish = offsets[position + 1]
    bucket_len = finish - start_at
    lead_shift = start_at - position * even_size
    tail_shift = finish - (position + 1) * even_size
    slot_ids = jnp.arange(bucket_cap, dtype=jnp.int32)
    in_bucket = slot_ids < bucket_len
    blocks = flat_part.reshape(local_experts, dp_count, even_size)
    received = lax.all_to_all(blocks, "dp", split_axis=1, concat_axis=1, tiled=True)
    row_sum = jnp.sum(received, axis=1, dtype=jnp.float32)
    tail_sums = row_sum[:, even_size - margin_size :]
    from_below = shifted(tail_sums, "dp", 1)
    extended = jnp.concatenate(
        [from_below, row_sum, zero_cols(local_experts, margin_size, jnp.float32)], axis=1
    )
    bucket_grad = cut_window(extended, lead_shift + margin_size, bucket_cap)
    bucket_grad = jnp.where(in_bucket[None, :], bucket_grad, 0.0)
    old_master = master[:, 0, :]
    moment_new = beta_one * moment_one[:, 0, :] + (1.0 - beta_one) * bucket_grad
    square_new = beta_two * moment_two[:, 0, :] + (1.0 - beta_two) * bucket_grad * bucket_grad
    update = (
        moment_new
        / (1.0 - beta_one**adam_step)
        / (jnp.sqrt(square_new / (1.0 - beta_two**adam_step)) + adam_eps)
    )
    master_new = old_master - learn_rate * (update + decay_rate * old_master)
    new_master = jnp.where(in_bucket[None, :], master_new, 0.0)
    new_moment_one = jnp.where(in_bucket[None, :], moment_new, 0.0)
    new_moment_two = jnp.where(in_bucket[None, :], square_new, 0.0)
    weight_half = new_master.astype(jnp.bfloat16)
    head_part = weight_half[:, :margin_size]
    from_above = shifted(head_part, "dp", -1)
    from_own = cut_window(weight_half, -lead_shift, even_size)
    from_next = cut_window(
        jnp.concatenate([zero_cols(local_experts, even_size, jnp.bfloat16), from_above], axis=1),
        -tail_shift,
        even_size,
    )
    new_weight = (from_own + from_next).reshape(local_experts, model_width // dp_count, 2 * hidden)
    return (
        new_master[:, None, :],
        new_moment_one[:, None, :],
        new_moment_two[:, None, :],
        new_weight,
        router_grad,
    )


def solution(mesh):
    placed = (
        P(("dp", "expert"), None),
        P(("dp", "expert"), None),
        P(("dp", "expert"), None, None),
        P(("dp", "expert"), None),
        P(("dp", "expert"), None),
        P("expert", "dp", None),
        P("expert", "dp", None),
        P("expert", "dp", None),
        P("expert", "dp", None),
        P(),
    )
    return jax.shard_map(
        shards,
        mesh=mesh,
        in_specs=placed,
        out_specs=(
            P("expert", "dp", None),
            P("expert", "dp", None),
            P("expert", "dp", None),
            P("expert", "dp", None),
            P(("dp", "expert"), None),
        ),
        check_vma=False,
    )
```

profile of v0, /device:TPU:1, one launch (start us, length us, event | category | flops | bytes accessed | tf_op | source)
XLA Modules:
  0.0 611.8 jit_solution(17735778480142060130)
XLA Ops:
  7.2 0.7 all-gather.2.cloned.1.call-update
  7.9 0.7 fusion.41
  8.8 0.8 select_reduce_fusion
  9.7 1.0 fusion.35
  10.7 0.6 copy.16
  11.3 7.6 %all-to-all-start.1 = ((bf16[16,1,16]{2,1,0:T(2,128)(2,1)}), bf16[16,1,16]{2,1,0:T(2,128)(2,1)S(1)}, u32[]{:S(2)}, u32[]{:S(2)}) async-start(bf16[16,1,16]{2,1,0:T(2,128)(2,1)} %copy.16), calls=%async_computation.1 | async-start | bytes 16384 | tf_op jit(solution)/shard_map/all_to_all | solution.py:72
  18.9 4.3 convolution_convert_fusion.1
  23.2 2.0 all-to-all-done.1
  25.2 4.6 all-to-all-start
  30.0 37.8 %all-to-all-done = bf16[16,16,6656]{2,1,0:T(8,128)(2,1)S(1)} async-done(((bf16[16,16,6656]{2,1,0:T(8,128)(2,1)}), bf16[16,16,6656]{2,1,0:T(8,128)(2,1)S(1)}, u32[]{:S(2)}, u32[]{:S(2)}) %all-to-all-start) | async-done | bytes 3407904 | tf_op jit(solution)/shard_map/all_to_all | solution.py:71
  67.8 22.0 %all-gather.2.cloned.1.call-done = bf16[1,768,2560]{2,1,0:T(8,128)(2,1)} async-done(((bf16[1,24,2560]{2,1,0:T(8,128)(2,1)}), bf16[1,768,2560]{2,1,0:T(8,128)(2,1)}) %all-gather.2.cloned.1.call-update) | async-done | bytes 3932176 | tf_op jit(solution)/shard_map/all_gather | solution.py:80
  89.8 4.6 fusion.31
  94.3 0.7 all_to_all.37
  95.0 6.3 %all-to-all-start.3 = ((f32[1,16,16]{2,0,1:T(1,128)}), f32[1,16,16]{2,0,1:T(1,128)S(1)}, u32[]{:S(2)}, u32[]{:S(2)}) async-start(f32[1,16,16]{2,0,1:T(1,128)} %all_to_all.37), calls=%async_computation.3 | async-start | bytes 16384 | tf_op jit(solution)/shard_map/all_to_all | solution.py:95
  101.4 6.5 %convolution_convert_fusion = bf16[2560,1536]{1,0:T(8,128)(2,1)} fusion(bf16[1,256,6656]{2,1,0:T(8,128)(2,1)S(1)} %bitcast.86, bf16[256,768]{1,0:T(8,128)(2,1)} %get-tuple-element.9, bf16[256,768]{1,0:T(8,128)(2,1)} %get-tuple-element.8), kind=kOutput, calls=%fused_computation.2 | convolution fusion | flops 2018770944 | bytes 9961472 | tf_op jit(solution)/shard_map/lrd,lrj->ldj/dot_general | solution.py:92
  107.8 21.6 %reshape_reshape.4 = bf16[1,32,122880]{2,0,1:T(2,128)(2,1)} reshape(bf16[2560,1536]{1,0:T(8,128)(2,1)} %convolution_convert_fusion) | data formatting | bytes 15728640 | tf_op jit(solution)/shard_map/reshape;reshape | solution.py:112
  130.0 49.5 %reduce.12 = bf16[32,122880]{1,0:T(8,128)(2,1)} reduce(bf16[32,1,122880]{2,1,0:T(2,128)(2,1)} %bitcast.84, bf16[]{:T(256)} %broadcast.208), dimensions={1}, to_apply=%bitcast.74.reduce_sub_computation | reduce | bytes 15728642
  179.5 10.4 %reshape.262 = bf16[32,2,61440]{2,1,0:T(2,128)(2,1)} reshape(bf16[32,122880]{1,0:T(8,128)(2,1)} %reduce.12) | data formatting | bytes 15728640
  189.9 8.7 %all-to-all-start.2 = ((bf16[32,2,61440]{2,1,0:T(2,128)(2,1)}), bf16[32,2,61440]{2,1,0:T(2,128)(2,1)}, u32[]{:S(2)}, u32[]{:S(2)}) async-start(bf16[32,2,61440]{2,1,0:T(2,128)(2,1)} %reshape.262), calls=%async_computation.2 | async-start | bytes 15728640 | tf_op jit(solution)/shard_map/all_to_all | solution.py:113
  198.7 0.6 fusion.58
  202.8 0.7 reduce.11
  203.6 1.3 gather_fusion
  204.9 332.9 %all-to-all-done.2 = bf16[32,2,61440]{2,1,0:T(2,128)(2,1)} async-done(((bf16[32,2,61440]{2,1,0:T(2,128)(2,1)}), bf16[32,2,61440]{2,1,0:T(2,128)(2,1)}, u32[]{:S(2)}, u32[]{:S(2)}) %all-to-all-start.2) | async-done | bytes 7864352 | tf_op jit(solution)/shard_map/all_to_all | solution.py:113
  537.8 23.3 %reshape.263 = bf16[32,1,122880]{2,1,0:T(2,128)(2,1)} reshape(bf16[32,2,61440]{2,1,0:T(2,128)(2,1)} %all-to-all-done.2) | data formatting | bytes 15728640
  561.1 16.2 %convert_reduce_fusion = f32[122880]{0:T(1024)S(1)} fusion(bf16[32,1,122880]{2,1,0:T(2,128)(2,1)} %reshape.263), kind=kLoop, calls=%fused_computation.1 | loop fusion | flops 7741440 | bytes 8355840 | tf_op jit(solution)/shard_map/reduce_sum | solution.py:114
  577.3 11.9 %collective-permute-start = (f32[1,3840]{1,0:T(1,128)S(1)}, f32[1,3840]{1,0:T(1,128)S(1)}, u32[]{:S(2)}, u32[]{:S(2)}) collective-permute-start(f32[1,3840]{1,0:T(1,128)S(1)} %slice.33), channel_id=1, source_target_pairs={{0,16},{16,32},{32,48},{48,64},{64,80},{80,96},{96,112},{112,128},... | collective-permute-start | bytes 46088 | tf_op jit(solution)/shard_map/ppermute | solution.py:17
  590.0 6.0 fusion.55
  596.0 1.9 collective-permute-start.1
  598.0 2.8 select_bitcast_fusion
  600.7 0.9 collective-permute-done.1
  601.6 2.3 fusion.29
  604.0 1.0 reshape.233
  (34 shorter events, 2.7 us)
Async XLA Ops:
  7.2 2.5 copy-start
  7.2 82.6 %all-gather.2.cloned.1.call-start = ((), (), s32[]{:S(2)}) async-start(), calls=%async_computation.4 | async-start | bytes 4055040 | tf_op jit(solution)/shard_map/all_gather | solution.py:80
  11.3 13.9 %all-to-all-start.1 = ((bf16[16,1,16]{2,1,0:T(2,128)(2,1)}), bf16[16,1,16]{2,1,0:T(2,128)(2,1)S(1)}, u32[]{:S(2)}, u32[]{:S(2)}) async-start(bf16[16,1,16]{2,1,0:T(2,128)(2,1)} %copy.16), calls=%async_computation.1 | async-start | bytes 16384 | tf_op jit(solution)/shard_map/all_to_all | solution.py:72
  25.2 42.5 %all-to-all-start = ((bf16[16,16,6656]{2,1,0:T(8,128)(2,1)}), bf16[16,16,6656]{2,1,0:T(8,128)(2,1)S(1)}, u32[]{:S(2)}, u32[]{:S(2)}) async-start(bf16[16,16,6656]{2,1,0:T(8,128)(2,1)} %bitcast.6), calls=%async_computation | async-start | bytes 6815744 | tf_op jit(solution)/shard_map/all_to_all | solution.py:71
  95.0 94.9 %all-to-all-start.3 = ((f32[1,16,16]{2,0,1:T(1,128)}), f32[1,16,16]{2,0,1:T(1,128)S(1)}, u32[]{:S(2)}, u32[]{:S(2)}) async-start(f32[1,16,16]{2,0,1:T(1,128)} %all_to_all.37), calls=%async_computation.3 | async-start | bytes 16384 | tf_op jit(solution)/shard_map/all_to_all | solution.py:95
  189.9 8.8 %copy-start.6 = (s32[33]{0:T(128)S(1)}, s32[33]{0:T(128)}, u32[]{:S(2)}) copy-start(s32[33]{0:T(128)} %param.19) | copy-start | bytes 400
  189.9 12.4 %copy-start.5 = (s32[128,1]{0,1:T(1,128)S(1)}, s32[128,1]{0,1:T(1,128)}, u32[]{:S(2)}) copy-start(s32[128,1]{0,1:T(1,128)} %param.14) | copy-start | bytes 1540
  189.9 347.9 %all-to-all-start.2 = ((bf16[32,2,61440]{2,1,0:T(2,128)(2,1)}), bf16[32,2,61440]{2,1,0:T(2,128)(2,1)}, u32[]{:S(2)}, u32[]{:S(2)}) async-start(bf16[32,2,61440]{2,1,0:T(2,128)(2,1)} %reshape.262), calls=%async_computation.2 | async-start | bytes 15728640 | tf_op jit(solution)/shard_map/all_to_all | solution.py:113
  561.1 28.9 %copy-start.2 = (f32[1,1,126720]{2,1,0:T(1,128)S(1)}, f32[1,1,126720]{2,1,0:T(1,128)}, u32[]{:S(2)}) copy-start(f32[1,1,126720]{2,1,0:T(1,128)} %param.18) | copy-start | bytes 1520644
  561.1 28.9 %copy-start.3 = (f32[1,1,126720]{2,1,0:T(1,128)S(1)}, f32[1,1,126720]{2,1,0:T(1,128)}, u32[]{:S(2)}) copy-start(f32[1,1,126720]{2,1,0:T(1,128)} %param.17) | copy-start | bytes 1520644
  561.1 28.9 %copy-start.4 = (f32[1,1,126720]{2,1,0:T(1,128)S(1)}, f32[1,1,126720]{2,1,0:T(1,128)}, u32[]{:S(2)}) copy-start(f32[1,1,126720]{2,1,0:T(1,128)} %param.16) | copy-start | bytes 1520644
  577.3 12.7 %collective-permute-start = (f32[1,3840]{1,0:T(1,128)S(1)}, f32[1,3840]{1,0:T(1,128)S(1)}, u32[]{:S(2)}, u32[]{:S(2)}) collective-permute-start(f32[1,3840]{1,0:T(1,128)S(1)} %slice.33), channel_id=1, source_target_pairs={{0,16},{16,32},{32,48},{48,64},{64,80},{80,96},{96,112},{112,128},... | collective-permute-start | bytes 46088 | tf_op jit(solution)/shard_map/ppermute | solution.py:17
  589.2 15.8 %copy-start.1 = (bf16[128,1]{0,1:T(2,128)(2,1)S(1)}, bf16[128,1]{0,1:T(2,128)(2,1)}, u32[]{:S(2)}) copy-start(bf16[128,1]{0,1:T(2,128)(2,1)} %param.13) | copy-start | bytes 772
  596.0 5.6 collective-permute-start.1
Sparse Core Ops, SparseCore 0:
  10.1 79.5 all-gather.1
where the time goes:
time: 614 us; the launch traced here: 612 us
  waiting for transfers between devices  397 us (65%)
  other arithmetic  79.8 us (13%)
  local copies, waits for them, and re-layouts  61.2 us (10%)
  starting transfers between devices  41.1 us (7%)
  between operations  16.9 us (3%)
  matrix products  16.3 us (3%)
    all_to_all x1, waiting for transfers between devices, shards(): lax.all_to_all(blocks, 'dp', split_axis=1, concat_axis=1, tiled=True)  333 us
    unnamed x1, other arithmetic  49.5 us
    all_to_all x1, waiting for transfers between devices, shards(): lax.all_to_all(packed, 'expert', split_axis=0, concat_axis=1, tiled=True)  37.8 us
    unnamed x17, local copies, waits for them, and re-layouts  34.3 us
    all_gather x1, waiting for transfers between devices, shards(): lax.all_gather(down_weight, 'dp', axis=1, tiled=True)  22 us
    another operation x1, local copies, waits for them, and re-layouts, shards(): blocks = flat_part.reshape(local_experts, dp_count, even_size)  21.6 us
    reduce_sum x1, other arithmetic, shards(): row_sum = jnp.sum(received, axis=1, dtype=jnp.float32)  16.2 us
    ppermute x2, starting transfers between devices, shifted(): return lax.ppermute(block, axis, route)  13.8 us
  transfers between devices with their start and end apart: 7, of which 6 were waited for; matrix products, arithmetic and copies ran while one was open for 17% of the time, Pallas kernels for 0%

commit v1 on v0

--- a/solution.py
+++ b/solution.py
@@ -1,6 +1,10 @@
+import functools
+
 import jax
 import jax.numpy as jnp
 from jax import lax
+from jax.experimental import pallas as pl
+from jax.experimental.pallas import tpu as pltpu
 from jax.sharding import PartitionSpec as P
 
 beta_one = 0.9
@@ -9,6 +13,203 @@
 decay_rate = 0.1
 adam_eps = 1e-08
 adam_step = 20.0
+
+MESH = pl.DeviceIdType.MESH
+
+
+def sum_kernel(
+    n,
+    feat_ref,
+    dgu_ref,
+    out_ref,
+    tail_ref,
+    feat_t,
+    own,
+    give,
+    sib,
+    work,
+    tail_in,
+    sib_send,
+    sib_recv,
+    ring_send,
+    ring_recv,
+    tail_send,
+    tail_recv,
+):
+    half = n // 2
+    rows, width = out_ref.shape
+    cols = width // 2
+    dp = lax.axis_index("dp")
+    expert = lax.axis_index("expert")
+    z, c = dp // 2, dp % 2
+    other = (z * 2 + 1 - c, expert)
+    ahead = (lax.rem(z + 1, n) * 2 + c, expert)
+    behind = (lax.rem(z + n - 1, n) * 2 + c, expert)
+    upper = (lax.rem(dp + 1, 2 * n), expert)
+    lower = (lax.rem(dp + 2 * n - 1, 2 * n), expert)
+
+    barrier = pltpu.get_barrier_semaphore()
+    for peer in (other, ahead, behind, upper, lower):
+        pl.semaphore_signal(barrier, inc=1, device_id=peer, device_id_type=MESH)
+
+    depth = feat_ref.shape[1]
+    for i in range(depth // 256):
+        feat_t[pl.ds(i * 256, 256), :] = feat_ref[:, pl.ds(i * 256, 256)].T
+
+    def sib_copy(r):
+        return pltpu.make_async_remote_copy(
+            src_ref=give.at[r],
+            dst_ref=sib.at[r],
+            send_sem=sib_send.at[r],
+            recv_sem=sib_recv.at[r],
+            device_id=other,
+            device_id_type=MESH,
+        )
+
+    def ring_copy(d, u, s):
+        return pltpu.make_async_remote_copy(
+            src_ref=work.at[d, u, s],
+            dst_ref=work.at[d, u, s + 1],
+            send_sem=ring_send.at[d, u, s],
+            recv_sem=ring_recv.at[d, u, s],
+            device_id=(ahead, behind)[d],
+            device_id_type=MESH,
+        )
+
+    def produce(places):
+        pieces = []
+        for r in places:
+            owner = lax.rem(z + r, n)
+            for side in (c, 1 - c):
+                start = pl.multiple_of((owner * 2 + side) * rows, 16)
+                pieces.append(feat_t[pl.ds(start, rows), :])
+        lhs = jnp.concatenate(pieces, axis=0)
+        for j in range(width // 256):
+            at = pl.ds(j * 256, 256)
+            prod = jnp.dot(lhs, dgu_ref[:, at], preferred_element_type=jnp.float32)
+            prod = prod.astype(jnp.bfloat16)
+            for i, r in enumerate(places):
+                own[r, :, at] = prod[2 * i * rows : (2 * i + 1) * rows]
+                give[r, :, at] = prod[(2 * i + 1) * rows : (2 * i + 2) * rows]
+
+    def chip_sum(r, u):
+        at = pl.ds(u * cols, cols)
+        return own[r, :, at].astype(jnp.float32) + sib[r, :, at].astype(jnp.float32)
+
+    def step(s, streams, fresh):
+        k = half - s
+        for d, u in streams:
+            r = k if d == 0 else n - k
+            total = chip_sum(r, u)
+            if (d, u) not in fresh:
+                ring_copy(d, u, s - 1).wait_recv()
+                total = total + work[d, u, s]
+            work[d, u, s] = total
+            ring_copy(d, u, s).start()
+
+    every = ((0, 0), (1, 1), (0, 1), (1, 0))
+    produce([half])
+    pl.semaphore_wait(barrier, 5)
+    sib_copy(half).start()
+    produce([half - 1, half + 1])
+    sib_copy(half - 1).start()
+    sib_copy(half + 1).start()
+    sib_copy(half).wait_recv()
+    step(0, every[:2], every[:2])
+
+    def body(s, _):
+        k = half - s
+        sib_copy(k).wait_recv()
+        sib_copy(n - k).wait_recv()
+
+        @pl.when(s == 1)
+        def _():
+            step(s, every, every[2:])
+
+        @pl.when(s > 1)
+        def _():
+            step(s, every, ())
+
+        @pl.when(k > 1)
+        def _():
+            produce([k - 1, n - k + 1])
+            sib_copy(k - 1).start()
+            sib_copy(n - k + 1).start()
+
+        return 0
+
+    lax.fori_loop(1, half, body, 0)
+    produce([0])
+    sib_copy(0).start()
+    sib_copy(0).wait_recv()
+    for u in range(2):
+        ring_copy(0, u, half - 1).wait_recv()
+        ring_copy(1, u, half - 1).wait_recv()
+        out_ref[:, pl.ds(u * cols, cols)] = chip_sum(0, u) + (work[0, u, half] + work[1, u, half])
+    last = pltpu.make_async_remote_copy(
+        src_ref=out_ref.at[pl.ds(rows - 8, 8)],
+        dst_ref=tail_in,
+        send_sem=tail_send,
+        recv_sem=tail_recv,
+        device_id=upper,
+        device_id_type=MESH,
+    )
+    last.start()
+
+    def drain(r, _):
+        sib_copy(r).wait_send()
+        return 0
+
+    lax.fori_loop(0, n, drain, 0)
+
+    def drain_ring(s, _):
+        for d, u in every:
+            ring_copy(d, u, s).wait_send()
+        return 0
+
+    for d, u in every[:2]:
+        ring_copy(d, u, 0).wait_send()
+    lax.fori_loop(1, half, drain_ring, 0)
+    last.wait()
+    tail_ref[...] = tail_in[...]
+
+
+def sum_over_slabs(features, dgu, n):
+    depth, width = features.shape[1], dgu.shape[1]
+    rows = depth // (2 * n)
+    half = n // 2
+    dma = pltpu.SemaphoreType.DMA
+    return pl.pallas_call(
+        functools.partial(sum_kernel, n),
+        out_shape=(
+            jax.ShapeDtypeStruct((rows, width), jnp.float32),
+            jax.ShapeDtypeStruct((8, width), jnp.float32),
+        ),
+        in_specs=[pl.BlockSpec(memory_space=pltpu.VMEM)] * 2,
+        out_specs=[pl.BlockSpec(memory_space=pltpu.VMEM)] * 2,
+        scratch_shapes=[
+            pltpu.VMEM((depth, features.shape[0]), jnp.bfloat16),
+            pltpu.VMEM((n, rows, width), jnp.bfloat16),
+            pltpu.VMEM((n, rows, width), jnp.bfloat16),
+            pltpu.VMEM((n, rows, width), jnp.bfloat16),
+            pltpu.VMEM((2, 2, half + 1, rows, width // 2), jnp.float32),
+            pltpu.VMEM((8, width), jnp.float32),
+            dma((n,)),
+            dma((n,)),
+            dma((2, 2, half)),
+            dma((2, 2, half)),
+            dma,
+            dma,
+        ],
+        compiler_params=pltpu.CompilerParams(
+            collective_id=0, has_side_effects=True, vmem_limit_bytes=40 * 2**20
+        ),
+        cost_estimate=pl.CostEstimate(
+            flops=2 * features.shape[0] * depth * width,
+            bytes_accessed=4 * depth * width,
+            transcendentals=0,
+        ),
+    )(features, dgu)
 
 
 def shifted(block, axis, distance):
@@ -89,16 +290,13 @@
     grad_gate = scaled * up_part * sigmoid_gate * (1.0 + gate_pre * (1.0 - sigmoid_gate))
     grad_up = scaled * gate_pre * sigmoid_gate
     grad_joined = jnp.concatenate([grad_gate, grad_up], axis=2).astype(jnp.bfloat16)
-    partial_sum = jnp.einsum(
-        "lrd,lrj->ldj", features, grad_joined, preferred_element_type=jnp.float32
-    ).astype(jnp.bfloat16)
+    row_block, below_rows = sum_over_slabs(features[0], grad_joined[0], dp_count // 2)
     returned = lax.all_to_all(scores, "expert", split_axis=1, concat_axis=0, tiled=True)
     flat_scores = returned.reshape(experts * capacity)
     router_grad = jnp.take(flat_scores, row_expert * capacity + row_slot).reshape(
         token_count, choice_count
     )
-    flat_size = partial_sum.shape[1] * partial_sum.shape[2]
-    flat_part = partial_sum.reshape(local_experts, flat_size)
+    flat_size = model_width * 2 * hidden
     even_size = flat_size // dp_count
     margin_size = bucket_cap - even_size
     position = lax.axis_index("dp")
@@ -109,11 +307,8 @@
     tail_shift = finish - (position + 1) * even_size
     slot_ids = jnp.arange(bucket_cap, dtype=jnp.int32)
     in_bucket = slot_ids < bucket_len
-    blocks = flat_part.reshape(local_experts, dp_count, even_size)
-    received = lax.all_to_all(blocks, "dp", split_axis=1, concat_axis=1, tiled=True)
-    row_sum = jnp.sum(received, axis=1, dtype=jnp.float32)
-    tail_sums = row_sum[:, even_size - margin_size :]
-    from_below = shifted(tail_sums, "dp", 1)
+    row_sum = row_block.reshape(1, even_size)
+    from_below = below_rows.reshape(1, -1)[:, -margin_size:]
     extended = jnp.concatenate(
         [from_below, row_sum, zero_cols(local_experts, margin_size, jnp.float32)], axis=1
     )

time: 614 us -> 222 us (0.36)
  waiting for transfers between devices: 397 us -> 58.3 us
  Pallas kernels: 0 us -> 90.2 us
  other arithmetic: 79.8 us -> 14.2 us
  local copies, waits for them, and re-layouts: 61.2 us -> 9.78 us
  starting transfers between devices: 41.1 us -> 22.2 us
  matrix products: 16.3 us -> 9.51 us
    all_to_all x1 -> x0, waiting for transfers between devices: 333 us -> none  [shards(): lax.all_to_all(blocks, 'dp', split_axis=1, concat_axis=1, tiled=True)]
    pallas_call x0 -> x1, Pallas kernels: none -> 90.2 us  [sum_over_slabs(): pl.pallas_call(functools.partial(sum_kernel, n), out_shape=(jax.ShapeDtyp...]
    unnamed x1 -> x0, other arithmetic: 49.5 us -> none
    unnamed x17 -> x18, local copies, waits for them, and re-layouts: 34.3 us -> 2.35 us
    another operation x1 -> x0, local copies, waits for them, and re-layouts: 21.6 us -> none  [shards(): blocks = flat_part.reshape(local_experts, dp_count, even_size)]
    reduce_sum x1 -> x0, other arithmetic: 16.2 us -> none  [shards(): row_sum = jnp.sum(received, axis=1, dtype=jnp.float32)]
    ppermute x2 -> x1, starting transfers between devices: 13.8 us -> 3.51 us  [shifted(): return lax.ppermute(block, axis, route)]
    all_to_all x1 -> x0, starting transfers between devices: 8.73 us -> none  [shards(): lax.all_to_all(blocks, 'dp', split_axis=1, concat_axis=1, tiled=True)]
  transfers between devices with their start and end apart: 7 -> 5, of which waited for: 6 -> 4; matrix products, arithmetic and copies ran while one was open for 17% -> 8% of each run, Pallas kernels for 0% -> 0%
where the time goes in v1:
time: 222 us; the launch traced here: 221 us
  Pallas kernels  90.2 us (41%)
  waiting for transfers between devices  58.3 us (26%)
  starting transfers between devices  22.2 us (10%)
  between operations  16.9 us (8%)
  other arithmetic  14.2 us (6%)
  local copies, waits for them, and re-layouts  9.78 us (4%)
  matrix products  9.51 us (4%)
    pallas_call x1, Pallas kernels, sum_over_slabs(): pl.pallas_call(functools.partial(sum_kernel, n), out_shape=(jax.ShapeDtyp...  90.2 us
    all_to_all x1, waiting for transfers between devices, shards(): lax.all_to_all(packed, 'expert', split_axis=0, concat_axis=1, tiled=True)  33.4 us
    all_gather x1, waiting for transfers between devices, shards(): lax.all_gather(down_weight, 'dp', axis=1, tiled=True)  18.7 us
    all_to_all x1, starting transfers between devices, shards(): lax.all_to_all(weight_sent, 'expert', split_axis=0, concat_axis=1, tiled=...  7.58 us
    all_to_all x1, starting transfers between devices, shards(): lax.all_to_all(scores, 'expert', split_axis=1, concat_axis=0, tiled=True)  6.36 us
    convert_element_type x1, other arithmetic, shards(): weight_half = new_master.astype(jnp.bfloat16)  5.99 us
    all_to_all x1, starting transfers between devices, shards(): lax.all_to_all(packed, 'expert', split_axis=0, concat_axis=1, tiled=True)  4.75 us
  transfers between devices with their start and end apart: 5, of which 4 were waited for; matrix products, arithmetic and copies ran while one was open for 8% of the time, Pallas kernels for 0%

profile of v1, /device:TPU:1, one launch (start us, length us, event | category | flops | bytes accessed | tf_op | source)
XLA Modules:
  0.0 221.1 jit_solution(16874012017852962437)
XLA Ops:
  7.2 0.7 all-gather.2.cloned.1.call-update
  7.9 0.7 fusion.38
  8.7 0.2 reduce_window_sum.11
  8.8 0.8 select_reduce_fusion
  9.7 1.0 fusion.32
  10.7 0.6 copy.15
  11.3 7.6 %all-to-all-start.1 = ((bf16[16,1,16]{2,1,0:T(2,128)(2,1)}), bf16[16,1,16]{2,1,0:T(2,128)(2,1)S(1)}, u32[]{:S(2)}, u32[]{:S(2)}) async-start(bf16[16,1,16]{2,1,0:T(2,128)(2,1)} %copy.15), calls=%async_computation.1 | async-start | bytes 16384 | tf_op jit(solution)/shard_map/all_to_all | solution.py:273
  18.9 4.3 %convolution_convert_fusion = bf16[256,6656]{1,0:T(8,128)(2,1)} fusion(bf16[128,1536]{1,0:T(8,128)(2,1)} %bitcast.91, bf16[128,2560]{1,0:T(8,128)(2,1)} %param.11, bf16[128,2560]{1,0:T(8,128)(2,1)} %param.10, s32[128]{0:T(128)S(1)} %select_reduce_fusion, s32[128]{0:T(128)} %bitcast.96, s32[256]{0:T(256)S(1)} %get-tuple-element.19, s32[256]{0:T(256)S(1)} %get-tuple-element.20), kind=kOutput, calls=%fused_computation.1 | convolution fusion | flops 443121664 | bytes 5114880 | tf_op jit(solution)/shard_map/dot_general | solution.py:267
  23.2 2.0 all-to-all-done.1
  25.2 4.8 %all-to-all-start = ((bf16[16,16,6656]{2,1,0:T(8,128)(2,1)}), bf16[16,16,6656]{2,1,0:T(8,128)(2,1)S(1)}, u32[]{:S(2)}, u32[]{:S(2)}) async-start(bf16[16,16,6656]{2,1,0:T(8,128)(2,1)} %bitcast.6), calls=%async_computation | async-start | bytes 6815744 | tf_op jit(solution)/shard_map/all_to_all | solution.py:272
  30.0 0.6 fusion.54
  33.3 1.1 reshape.257
  34.5 0.1 reshape.234
  34.5 33.4 %all-to-all-done = bf16[16,16,6656]{2,1,0:T(8,128)(2,1)S(1)} async-done(((bf16[16,16,6656]{2,1,0:T(8,128)(2,1)}), bf16[16,16,6656]{2,1,0:T(8,128)(2,1)S(1)}, u32[]{:S(2)}, u32[]{:S(2)}) %all-to-all-start) | async-done | bytes 3407904 | tf_op jit(solution)/shard_map/all_to_all | solution.py:272
  67.9 1.7 copy-done.1
  69.7 1.4 slice_bitcast_fusion.2.feat_ref
  71.1 18.7 %all-gather.2.cloned.1.call-done = bf16[1,768,2560]{2,1,0:T(8,128)(2,1)} async-done(((bf16[1,24,2560]{2,1,0:T(8,128)(2,1)}), bf16[1,768,2560]{2,1,0:T(8,128)(2,1)}) %all-gather.2.cloned.1.call-update) | async-done | bytes 3932176 | tf_op jit(solution)/shard_map/all_gather | solution.py:281
  89.8 4.2 %fusion.28 = (bf16[256,768]{1,0:T(8,128)(2,1)S(1)}, bf16[256,768]{1,0:T(8,128)(2,1)S(1)}, f32[256]{0:T(256)S(1)}) fusion(f32[256]{0:T(256)S(1)} %reshape.234, bf16[1,256,6656]{2,1,0:T(8,128)(2,1)} %bitcast.88, bf16[1,768,2560]{2,1,0:T(8,128)(2,1)} %all-gather.2.cloned.1.call-done), kind=kOutput, calls=%fused_computation.49 | convolution fusion | flops 1010564864 | bytes 6817792 | tf_op jit(solution)/shard_map/lrd,lkd->lrk/dot_general | solution.py:278
  94.1 90.2 %shard_map.137 = (f32[80,1536]{1,0:T(8,128)S(1)}, f32[8,1536]{1,0:T(8,128)S(1)}) custom-call(bf16[256,2560]{1,0:T(8,128)(2,1)S(1)} %slice_bitcast_fusion.2.feat_ref, bf16[256,1536]{1,0:T(8,128)(2,1)S(1)} %pad_maximum_fusion.dgu_ref), custom_call_target="tpu_custom_call" | custom-call | flops 2013265920 | bytes 15728640 | tf_op jit(solution)/shard_map/pallas_call | solution.py:182
  184.3 0.5 copy.18
  185.0 6.0 %fusion.51 = (bf16[1,126720]{1,0:T(2,128)(2,1)S(1)}, f32[1,126720]{1,0:T(1,128)}, f32[1,126720]{1,0:T(1,128)S(1)}) fusion(f32[1,1,126720]{2,1,0:T(1,128)S(1)} %copy-done.3, f32[1,1,126720]{2,1,0:T(1,128)S(1)} %copy-done.4, f32[1,1,126720]{2,1,0:T(1,128)S(1)} %copy-done.5, s32[]{:T(128)S(6)} %sub.26, f32[1,130560]{1,0:T(1,128)S(1)} %copy-done.2, ...), kind=kLoop, calls=%fused_computation.90 | loop fusion | flops 2661120 | bytes 3801608 | tf_op jit(solution)/shard_map/convert_element_type | solution.py:329
  191.0 3.5 %collective-permute-start = (bf16[1,3840]{1,0:T(2,128)(2,1)S(1)}, bf16[1,3840]{1,0:T(2,128)(2,1)S(1)}, u32[]{:S(2)}, u32[]{:S(2)}) collective-permute-start(bf16[1,3840]{1,0:T(2,128)(2,1)S(1)} %slice.34), channel_id=1, source_target_pairs={{16,0},{32,16},{48,32},{64,48},{80,64},{96,80},{112,96},{128,112},... | collective-permute-start | bytes 23048 | tf_op jit(solution)/shard_map/ppermute | solution.py:218
  194.5 0.7 all_to_all.33
  195.2 6.4 %all-to-all-start.2 = ((f32[1,16,16]{2,0,1:T(1,128)}), f32[1,16,16]{2,0,1:T(1,128)S(1)}, u32[]{:S(2)}, u32[]{:S(2)}) async-start(f32[1,16,16]{2,0,1:T(1,128)} %all_to_all.33), calls=%async_computation.2 | async-start | bytes 16384 | tf_op jit(solution)/shard_map/all_to_all | solution.py:294
  201.6 2.8 %select_bitcast_fusion = (f32[1,1,126720]{2,1,0:T(1,128)}, f32[1,1,126720]{2,1,0:T(1,128)}) fusion(s32[]{:T(128)S(6)} %sub.26, f32[1,126720]{1,0:T(1,128)S(1)} %get-tuple-element.11, f32[1,1,126720]{2,1,0:T(1,128)S(1)} %copy-done.3, f32[1,1,126720]{2,1,0:T(1,128)S(1)} %copy-done.4), kind=kLoop, calls=%fused_computation.42 | loop fusion | flops 1267200 | bytes 2534404 | tf_op jit(solution)/shard_map/broadcast_in_dim | solution.py:342
  204.3 3.5 %all-to-all-done.2 = f32[1,16,16]{2,0,1:T(1,128)S(1)} async-done(((f32[1,16,16]{2,0,1:T(1,128)}), f32[1,16,16]{2,0,1:T(1,128)S(1)}, u32[]{:S(2)}, u32[]{:S(2)}) %all-to-all-start.2) | async-done | bytes 1056 | tf_op jit(solution)/shard_map/all_to_all | solution.py:294
  207.9 0.5 broadcast.206
  208.4 0.7 reduce.10
  209.1 1.3 gather_fusion
  210.4 0.5 and_select_fusion
  210.9 2.4 %fusion.26 = bf16[122880]{0:T(1024)(128)(2,1)S(1)} fusion(s32[]{:T(128)S(6)} %select_n.80, bf16[1,3840]{1,0:T(2,128)(2,1)S(1)} %collective-permute-done, bf16[1,126720]{1,0:T(2,128)(2,1)S(1)} %get-tuple-element.9, s32[]{:T(128)S(6)} %select_n.79), kind=kLoop, calls=%fused_computation.47 | loop fusion | flops 491520 | bytes 499208 | tf_op jit(solution)/shard_map/add | solution.py:338
  213.3 1.0 reshape.232
  (30 shorter events, 0.4 us)
Async XLA Ops:
  7.2 2.5 %copy-start = (bf16[128,1]{0,1:T(2,128)(2,1)S(1)}, bf16[128,1]{0,1:T(2,128)(2,1)}, u32[]{:S(2)}) copy-start(bf16[128,1]{0,1:T(2,128)(2,1)} %param.13) | copy-start | bytes 772
  7.2 82.6 %all-gather.2.cloned.1.call-start = ((), (), s32[]{:S(2)}) async-start(), calls=%async_computation.3 | async-start | bytes 4055040 | tf_op jit(solution)/shard_map/all_gather | solution.py:281
  11.3 13.9 %all-to-all-start.1 = ((bf16[16,1,16]{2,1,0:T(2,128)(2,1)}), bf16[16,1,16]{2,1,0:T(2,128)(2,1)S(1)}, u32[]{:S(2)}, u32[]{:S(2)}) async-start(bf16[16,1,16]{2,1,0:T(2,128)(2,1)} %copy.15), calls=%async_computation.1 | async-start | bytes 16384 | tf_op jit(solution)/shard_map/all_to_all | solution.py:273
  25.2 4.8 %copy-start.7 = (s32[33]{0:T(128)S(1)}, s32[33]{0:T(128)}, u32[]{:S(2)}) copy-start(s32[33]{0:T(128)} %param.19) | copy-start | bytes 400
  25.2 9.2 %copy-start.6 = (s32[128,1]{0,1:T(1,128)S(1)}, s32[128,1]{0,1:T(1,128)}, u32[]{:S(2)}) copy-start(s32[128,1]{0,1:T(1,128)} %param.14) | copy-start | bytes 1540
  25.2 42.7 %all-to-all-start = ((bf16[16,16,6656]{2,1,0:T(8,128)(2,1)}), bf16[16,16,6656]{2,1,0:T(8,128)(2,1)S(1)}, u32[]{:S(2)}, u32[]{:S(2)}) async-start(bf16[16,16,6656]{2,1,0:T(8,128)(2,1)} %bitcast.6), calls=%async_computation | async-start | bytes 6815744 | tf_op jit(solution)/shard_map/all_to_all | solution.py:272
  67.9 1.8 copy-start.1
  94.1 90.9 %copy-start.2 = (f32[1,130560]{1,0:T(1,128)S(1)}, f32[1,130560]{1,0:T(1,128)}, u32[]{:S(2)}) copy-start(f32[1,130560]{1,0:T(1,128)} %reshape.257) | copy-start | bytes 1566724
  94.1 90.9 %copy-start.3 = (f32[1,1,126720]{2,1,0:T(1,128)S(1)}, f32[1,1,126720]{2,1,0:T(1,128)}, u32[]{:S(2)}) copy-start(f32[1,1,126720]{2,1,0:T(1,128)} %param.18) | copy-start | bytes 1520644
  94.1 90.9 %copy-start.4 = (f32[1,1,126720]{2,1,0:T(1,128)S(1)}, f32[1,1,126720]{2,1,0:T(1,128)}, u32[]{:S(2)}) copy-start(f32[1,1,126720]{2,1,0:T(1,128)} %param.17) | copy-start | bytes 1520644
  94.1 90.9 %copy-start.5 = (f32[1,1,126720]{2,1,0:T(1,128)S(1)}, f32[1,1,126720]{2,1,0:T(1,128)}, u32[]{:S(2)}) copy-start(f32[1,1,126720]{2,1,0:T(1,128)} %param.16) | copy-start | bytes 1520644
  191.0 20.0 %collective-permute-start = (bf16[1,3840]{1,0:T(2,128)(2,1)S(1)}, bf16[1,3840]{1,0:T(2,128)(2,1)S(1)}, u32[]{:S(2)}, u32[]{:S(2)}) collective-permute-start(bf16[1,3840]{1,0:T(2,128)(2,1)S(1)} %slice.34), channel_id=1, source_target_pairs={{16,0},{32,16},{48,32},{64,48},{80,64},{96,80},{112,96},{128,112},... | collective-permute-start | bytes 23048 | tf_op jit(solution)/shard_map/ppermute | solution.py:218
  195.2 12.7 %all-to-all-start.2 = ((f32[1,16,16]{2,0,1:T(1,128)}), f32[1,16,16]{2,0,1:T(1,128)S(1)}, u32[]{:S(2)}, u32[]{:S(2)}) async-start(f32[1,16,16]{2,0,1:T(1,128)} %all_to_all.33), calls=%async_computation.2 | async-start | bytes 16384 | tf_op jit(solution)/shard_map/all_to_all | solution.py:294
Sparse Core Ops, SparseCore 0:
  10.1 79.5 all-gather.1

commit v2 on v1

--- a/solution.py
+++ b/solution.py
@@ -17,44 +17,391 @@
 MESH = pl.DeviceIdType.MESH
 
 
+def expert_peers(experts):
+    side = 4 if experts % 4 == 0 else experts
+    me = lax.axis_index("expert")
+
+    def peer(i):
+        x = lax.rem(me // side + i // side, experts // side)
+        return x * side + lax.rem(me % side + i % side, side)
+
+    return me, peer
+
+
+def send_kernel(
+    n,
+    experts,
+    tok_ref,
+    grad_ref,
+    saved_ref,
+    weight_ref,
+    route_ref,
+    down_ref,
+    feat_ref,
+    dgu_ref,
+    score_ref,
+    target_ref,
+    pack_one,
+    pack_two,
+    rows_in,
+    down_wide,
+    down_sib,
+    down_all,
+    one_send,
+    one_recv,
+    two_send,
+    two_recv,
+    ring_send,
+    ring_recv,
+    pass_send,
+    pass_recv,
+    first_send,
+    first_recv,
+):
+    half = n // 2
+    count, width = tok_ref.shape
+    hidden = saved_ref.shape[1] // 2
+    slots = feat_ref.shape[0] // experts
+    share = down_ref.shape[0]
+    cols = width // 2
+    dp = lax.axis_index("dp")
+    me, peer = expert_peers(experts)
+    z, c = dp // 2, dp % 2
+    other = (z * 2 + 1 - c, me)
+    ahead = (lax.rem(z + 1, n) * 2 + c, me)
+    behind = (lax.rem(z + n - 1, n) * 2 + c, me)
+
+    barrier = pltpu.get_barrier_semaphore()
+    for device in (other, ahead, behind):
+        pl.semaphore_signal(barrier, inc=1, device_id=device, device_id_type=MESH)
+
+    def greet(i, _):
+        pl.semaphore_signal(barrier, inc=1, device_id=(dp, peer(i)), device_id_type=MESH)
+        return 0
+
+    lax.fori_loop(1, experts, greet, 0)
+    down_wide[...] = down_ref[...].astype(jnp.float32)
+    pl.semaphore_wait(barrier, experts + 2)
+
+    first = pltpu.make_async_remote_copy(
+        src_ref=down_wide.at[:, pl.ds(pl.multiple_of((1 - c) * cols, 128), cols)],
+        dst_ref=down_sib,
+        send_sem=first_send,
+        recv_sem=first_recv,
+        device_id=other,
+        device_id_type=MESH,
+    )
+    first.start()
+
+    def place(idx):
+        return pl.ds(pl.multiple_of(lax.rem(idx + n, n) * 2 * share, 16), 2 * share)
+
+    def ring_copy(d, s, split):
+        idx = z - s if d == 0 else z + s
+        at = pl.ds(d * (cols // 2), cols // 2) if split else pl.ds(0, cols)
+        block = down_all.at[c, place(idx), at]
+        return pltpu.make_async_remote_copy(
+            src_ref=block,
+            dst_ref=block,
+            send_sem=ring_send.at[d, s],
+            recv_sem=ring_recv.at[d, s],
+            device_id=(ahead, behind)[d],
+            device_id_type=MESH,
+        )
+
+    def arrival(d, s, split):
+        idx = z - s - 1 if d == 0 else z + s + 1
+        at = pl.ds(d * (cols // 2), cols // 2) if split else pl.ds(0, cols)
+        block = down_all.at[c, place(idx), at]
+        return pltpu.make_async_remote_copy(
+            src_ref=block,
+            dst_ref=block,
+            send_sem=ring_send.at[d, s],
+            recv_sem=ring_recv.at[d, s],
+            device_id=(ahead, behind)[d],
+            device_id_type=MESH,
+        )
+
+    def pass_copy(r, side):
+        block = down_all.at[side, place(z + r), pl.ds(0, cols)]
+        return pltpu.make_async_remote_copy(
+            src_ref=block,
+            dst_ref=block,
+            send_sem=pass_send.at[r],
+            recv_sem=pass_recv.at[r],
+            device_id=other,
+            device_id_type=MESH,
+        )
+
+    route = route_ref[...]
+    expert_id = lax.broadcasted_iota(jnp.int32, (experts, count), 0)
+    onehot = jnp.where(route == expert_id, 1.0, 0.0)
+    before = lax.broadcasted_iota(jnp.int32, (count, count), 0)
+    after = lax.broadcasted_iota(jnp.int32, (count, count), 1)
+    upper = jnp.where(before < after, 1.0, 0.0).astype(jnp.bfloat16)
+    earlier = jnp.dot(onehot.astype(jnp.bfloat16), upper, preferred_element_type=jnp.float32)
+    slot = jnp.sum(earlier * onehot, axis=0, keepdims=True).astype(jnp.int32)
+    target = route * slots + slot
+    target_ref[...] = target
+    slot_id = lax.broadcasted_iota(jnp.int32, (experts * slots, count), 0)
+    select = jnp.where(slot_id == target, 1.0, 0.0).astype(jnp.bfloat16)
+
+    def pack(into, at, values):
+        into[:, pl.ds(at, values.shape[1])] = jnp.dot(
+            select, values, preferred_element_type=jnp.float32
+        ).astype(jnp.bfloat16)
+
+    def block(e):
+        return pl.ds(pl.multiple_of(e * slots, 16), slots)
+
+    def one_copy(i):
+        return pltpu.make_async_remote_copy(
+            src_ref=pack_one.at[block(peer(i))],
+            dst_ref=rows_in.at[block(me)],
+            send_sem=one_send.at[i],
+            recv_sem=one_recv.at[i],
+            device_id=(dp, peer(i)),
+            device_id_type=MESH,
+        )
+
+    def two_copy(i):
+        return pltpu.make_async_remote_copy(
+            src_ref=pack_two.at[block(peer(i))],
+            dst_ref=feat_ref.at[block(me)],
+            send_sem=two_send.at[i],
+            recv_sem=two_recv.at[i],
+            device_id=(dp, peer(i)),
+            device_id_type=MESH,
+        )
+
+    step = 256 if width % 256 == 0 else width
+    for j in range(width // step):
+        pack(pack_one, j * step, grad_ref[:, pl.ds(j * step, step)])
+    for j in range(2 * hidden // 256):
+        pack(pack_one, width + j * 256, saved_ref[:, pl.ds(j * 256, 256)])
+    wide = jnp.broadcast_to(weight_ref[...].astype(jnp.float32), (count, 128))
+    pack(pack_one, width + 2 * hidden, wide.astype(jnp.bfloat16))
+
+    first.wait()
+    mine = down_wide[:, pl.ds(pl.multiple_of(c * cols, 128), cols)]
+    theirs = down_sib[...]
+    top, low = jnp.where(c == 0, mine, theirs), jnp.where(c == 0, theirs, mine)
+    down_all[c, place(z), :] = jnp.concatenate([top, low], axis=0).astype(jnp.bfloat16)
+    ring_copy(0, 0, half == 1).start()
+    ring_copy(1, 0, half == 1).start()
+
+    def send_one(i, _):
+        one_copy(i).start()
+        return 0
+
+    lax.fori_loop(1, experts, send_one, 0)
+    pass_copy(0, c).start()
+    for j in range(width // step):
+        pack(pack_two, j * step, tok_ref[:, pl.ds(j * step, step)])
+
+    def send_two(i, _):
+        two_copy(i).start()
+        return 0
+
+    lax.fori_loop(1, experts, send_two, 0)
+    rows_in[block(me), :] = pack_one[block(me), :]
+    feat_ref[block(me), :] = pack_two[block(me), :]
+
+    def forward(s, _):
+        arrival(0, s - 1, False).wait_recv()
+        arrival(1, s - 1, False).wait_recv()
+
+        @pl.when(s < half - 1)
+        def _():
+            ring_copy(0, s, False).start()
+            ring_copy(1, s, False).start()
+
+        @pl.when(s == half - 1)
+        def _():
+            ring_copy(0, s, True).start()
+            ring_copy(1, s, True).start()
+
+        pass_copy(n - s, c).start()
+        pass_copy(s, c).start()
+        return 0
+
+    lax.fori_loop(1, half, forward, 0)
+    arrival(0, half - 1, True).wait_recv()
+    arrival(1, half - 1, True).wait_recv()
+    pass_copy(half, c).start()
+
+    def land_one(i, _):
+        one_copy(i).wait_recv()
+        return 0
+
+    lax.fori_loop(1, experts, land_one, 0)
+
+    def land_pass(r, _):
+        pass_copy(r, 1 - c).wait_recv()
+        return 0
+
+    lax.fori_loop(0, n, land_pass, 0)
+
+    tile = 256 if hidden % 256 == 0 else hidden
+    weight = rows_in[:, pl.ds(width + 2 * hidden, 128)].astype(jnp.float32)[:, :1]
+    score = jnp.zeros((experts * slots, 1), jnp.float32)
+    for j in range(hidden // tile):
+        back = sum(
+            lax.dot_general(
+                rows_in[:, pl.ds(side * cols, cols)],
+                down_all[side, pl.ds(j * tile, tile), :],
+                (((1,), (1,)), ((), ())),
+                preferred_element_type=jnp.float32,
+            )
+            for side in range(2)
+        )
+        gate = rows_in[:, pl.ds(width + j * tile, tile)].astype(jnp.float32)
+        up = rows_in[:, pl.ds(width + hidden + j * tile, tile)].astype(jnp.float32)
+        sig = 1.0 / (1.0 + jnp.exp(-gate))
+        silu = gate * sig
+        score = score + jnp.sum(silu * up * back, axis=1, keepdims=True)
+        scaled = weight * back
+        dgu_ref[:, pl.ds(j * tile, tile)] = (
+            scaled * up * sig * (1.0 + gate * (1.0 - sig))
+        ).astype(jnp.bfloat16)
+        dgu_ref[:, pl.ds(hidden + j * tile, tile)] = (scaled * silu).astype(jnp.bfloat16)
+    score_ref[...] = jnp.broadcast_to(score, score_ref.shape)
+
+    def finish(i, _):
+        one_copy(i).wait_send()
+        two_copy(i).wait()
+        return 0
+
+    lax.fori_loop(1, experts, finish, 0)
+
+    def finish_pass(r, _):
+        pass_copy(r, c).wait_send()
+        return 0
+
+    lax.fori_loop(0, n, finish_pass, 0)
+
+    def finish_ring(s, _):
+        ring_copy(0, s, False).wait_send()
+        ring_copy(1, s, False).wait_send()
+        return 0
+
+    lax.fori_loop(0, half - 1, finish_ring, 0)
+    ring_copy(0, half - 1, True).wait_send()
+    ring_copy(1, half - 1, True).wait_send()
+
+
+def rows_to_experts(tokens, out_grad, saved, weight, routes, down, n, experts, slots):
+    count, width = tokens.shape
+    hidden = saved.shape[1] // 2
+    total = experts * slots
+    half = n // 2
+    wide = width + 2 * hidden + 128
+    dma = pltpu.SemaphoreType.DMA
+    bf16, f32 = jnp.bfloat16, jnp.float32
+    return pl.pallas_call(
+        functools.partial(send_kernel, n, experts),
+        out_shape=(
+            jax.ShapeDtypeStruct((total, width), bf16),
+            jax.ShapeDtypeStruct((total, 2 * hidden), bf16),
+            jax.ShapeDtypeStruct((total, count), f32),
+            jax.ShapeDtypeStruct((1, count), jnp.int32),
+        ),
+        in_specs=[pl.BlockSpec(memory_space=pltpu.VMEM)] * 6,
+        out_specs=[pl.BlockSpec(memory_space=pltpu.VMEM)] * 4,
+        scratch_shapes=[
+            pltpu.VMEM((total, wide), bf16),
+            pltpu.VMEM((total, width), bf16),
+            pltpu.VMEM((total, wide), bf16),
+            pltpu.VMEM(down.shape, f32),
+            pltpu.VMEM((down.shape[0], width // 2), f32),
+            pltpu.VMEM((2, hidden, width // 2), bf16),
+            dma((experts,)),
+            dma((experts,)),
+            dma((experts,)),
+            dma((experts,)),
+            dma((2, half)),
+            dma((2, half)),
+            dma((n,)),
+            dma((n,)),
+            dma,
+            dma,
+        ],
+        compiler_params=pltpu.CompilerParams(
+            collective_id=1, has_side_effects=True, vmem_limit_bytes=32 * 2**20
+        ),
+        cost_estimate=pl.CostEstimate(
+            flops=2 * total * (width * hidden + count * wide),
+            bytes_accessed=4 * total * wide,
+            transcendentals=total * hidden,
+        ),
+    )(tokens, out_grad, saved, weight, routes.reshape(1, count), down)
+
+
 def sum_kernel(
     n,
+    experts,
     feat_ref,
     dgu_ref,
+    score_ref,
+    target_ref,
     out_ref,
     tail_ref,
+    router_ref,
     feat_t,
     own,
     give,
     sib,
     work,
+    scale,
     tail_in,
+    score_in,
     sib_send,
     sib_recv,
     ring_send,
     ring_recv,
+    scale_send,
+    scale_recv,
+    score_send,
+    score_recv,
     tail_send,
     tail_recv,
 ):
     half = n // 2
     rows, width = out_ref.shape
     cols = width // 2
+    slots = score_ref.shape[0] // experts
     dp = lax.axis_index("dp")
-    expert = lax.axis_index("expert")
+    me, peer = expert_peers(experts)
     z, c = dp // 2, dp % 2
-    other = (z * 2 + 1 - c, expert)
-    ahead = (lax.rem(z + 1, n) * 2 + c, expert)
-    behind = (lax.rem(z + n - 1, n) * 2 + c, expert)
-    upper = (lax.rem(dp + 1, 2 * n), expert)
-    lower = (lax.rem(dp + 2 * n - 1, 2 * n), expert)
+    other = (z * 2 + 1 - c, me)
+    ahead = (lax.rem(z + 1, n) * 2 + c, me)
+    behind = (lax.rem(z + n - 1, n) * 2 + c, me)
+    upper = (lax.rem(dp + 1, 2 * n), me)
+    lower = (lax.rem(dp + 2 * n - 1, 2 * n), me)
 
     barrier = pltpu.get_barrier_semaphore()
-    for peer in (other, ahead, behind, upper, lower):
-        pl.semaphore_signal(barrier, inc=1, device_id=peer, device_id_type=MESH)
+    for device in (other, ahead, behind, upper, lower):
+        pl.semaphore_signal(barrier, inc=1, device_id=device, device_id_type=MESH)
+
+    def greet(i, _):
+        pl.semaphore_signal(barrier, inc=1, device_id=(dp, peer(i)), device_id_type=MESH)
+        return 0
+
+    lax.fori_loop(1, experts, greet, 0)
 
     depth = feat_ref.shape[1]
     for i in range(depth // 256):
         feat_t[pl.ds(i * 256, 256), :] = feat_ref[:, pl.ds(i * 256, 256)].T
+
+    def score_copy(i):
+        return pltpu.make_async_remote_copy(
+            src_ref=score_ref.at[pl.ds(pl.multiple_of(peer(i) * slots, 8), slots)],
+            dst_ref=score_in.at[pl.ds(pl.multiple_of(me * slots, 8), slots)],
+            send_sem=score_send.at[i],
+            recv_sem=score_recv.at[i],
+            device_id=(dp, peer(i)),
+            device_id_type=MESH,
+        )
 
     def sib_copy(r):
         return pltpu.make_async_remote_copy(
@@ -67,14 +414,20 @@
         )
 
     def ring_copy(d, u, s):
-        return pltpu.make_async_remote_copy(
-            src_ref=work.at[d, u, s],
-            dst_ref=work.at[d, u, s + 1],
-            send_sem=ring_send.at[d, u, s],
-            recv_sem=ring_recv.at[d, u, s],
-            device_id=(ahead, behind)[d],
-            device_id_type=MESH,
-        )
+        return [
+            pltpu.make_async_remote_copy(
+                src_ref=buffer.at[d, u, s],
+                dst_ref=buffer.at[d, u, s + 1],
+                send_sem=send.at[d, u, s],
+                recv_sem=recv.at[d, u, s],
+                device_id=(ahead, behind)[d],
+                device_id_type=MESH,
+            )
+            for buffer, send, recv in (
+                (work, ring_send, ring_recv),
+                (scale, scale_send, scale_recv),
+            )
+        ]
 
     def produce(places):
         pieces = []
@@ -96,20 +449,28 @@
         at = pl.ds(u * cols, cols)
         return own[r, :, at].astype(jnp.float32) + sib[r, :, at].astype(jnp.float32)
 
+    def decoded(d, u, s):
+        return work[d, u, s].astype(jnp.int32).astype(jnp.float32) * scale[d, u, s]
+
     def step(s, streams, fresh):
         k = half - s
         for d, u in streams:
             r = k if d == 0 else n - k
             total = chip_sum(r, u)
             if (d, u) not in fresh:
-                ring_copy(d, u, s - 1).wait_recv()
-                total = total + work[d, u, s]
-            work[d, u, s] = total
-            ring_copy(d, u, s).start()
+                for copy in ring_copy(d, u, s - 1):
+                    copy.wait_recv()
+                total = total + decoded(d, u, s)
+            most = jnp.maximum(jnp.max(jnp.abs(total), axis=0, keepdims=True), 1e-30)
+            scale[d, u, s] = most * (1.0 / 32767.0)
+            coded = jnp.round(total * (32767.0 / most))
+            work[d, u, s] = coded.astype(jnp.int32).astype(jnp.int16)
+            for copy in ring_copy(d, u, s):
+                copy.start()
 
     every = ((0, 0), (1, 1), (0, 1), (1, 0))
     produce([half])
-    pl.semaphore_wait(barrier, 5)
+    pl.semaphore_wait(barrier, experts + 4)
     sib_copy(half).start()
     produce([half - 1, half + 1])
     sib_copy(half - 1).start()
@@ -117,6 +478,14 @@
     sib_copy(half).wait_recv()
     step(0, every[:2], every[:2])
 
+    def send_score(i, _):
+        score_copy(i).start()
+        return 0
+
+    lax.fori_loop(1, experts, send_score, 0)
+    mine = pl.ds(pl.multiple_of(me * slots, 8), slots)
+    score_in[mine, :] = score_ref[mine, :]
+
     def body(s, _):
         k = half - s
         sib_copy(k).wait_recv()
@@ -141,11 +510,24 @@
     lax.fori_loop(1, half, body, 0)
     produce([0])
     sib_copy(0).start()
+
+    def land_score(i, _):
+        score_copy(i).wait()
+        return 0
+
+    lax.fori_loop(1, experts, land_score, 0)
+    slot_id = lax.broadcasted_iota(jnp.int32, score_in.shape, 0)
+    router_ref[...] = jnp.sum(
+        jnp.where(slot_id == target_ref[...], score_in[...], 0.0), axis=0, keepdims=True
+    )
     sib_copy(0).wait_recv()
     for u in range(2):
-        ring_copy(0, u, half - 1).wait_recv()
-        ring_copy(1, u, half - 1).wait_recv()
-        out_ref[:, pl.ds(u * cols, cols)] = chip_sum(0, u) + (work[0, u, half] + work[1, u, half])
+        for d in range(2):
+            for copy in ring_copy(d, u, half - 1):
+                copy.wait_recv()
+        out_ref[:, pl.ds(u * cols, cols)] = chip_sum(0, u) + (
+            decoded(0, u, half) + decoded(1, u, half)
+        )
     last = pltpu.make_async_remote_copy(
         src_ref=out_ref.at[pl.ds(rows - 8, 8)],
         dst_ref=tail_in,
@@ -164,40 +546,49 @@
 
     def drain_ring(s, _):
         for d, u in every:
-            ring_copy(d, u, s).wait_send()
+            for copy in ring_copy(d, u, s):
+                copy.wait_send()
         return 0
 
     for d, u in every[:2]:
-        ring_copy(d, u, 0).wait_send()
+        for copy in ring_copy(d, u, 0):
+            copy.wait_send()
     lax.fori_loop(1, half, drain_ring, 0)
     last.wait()
     tail_ref[...] = tail_in[...]
 
 
-def sum_over_slabs(features, dgu, n):
+def sum_over_slabs(features, dgu, scores, targets, n, experts):
     depth, width = features.shape[1], dgu.shape[1]
     rows = depth // (2 * n)
     half = n // 2
     dma = pltpu.SemaphoreType.DMA
     return pl.pallas_call(
-        functools.partial(sum_kernel, n),
+        functools.partial(sum_kernel, n, experts),
         out_shape=(
             jax.ShapeDtypeStruct((rows, width), jnp.float32),
             jax.ShapeDtypeStruct((8, width), jnp.float32),
+            jax.ShapeDtypeStruct(targets.shape, jnp.float32),
         ),
-        in_specs=[pl.BlockSpec(memory_space=pltpu.VMEM)] * 2,
-        out_specs=[pl.BlockSpec(memory_space=pltpu.VMEM)] * 2,
+        in_specs=[pl.BlockSpec(memory_space=pltpu.VMEM)] * 4,
+        out_specs=[pl.BlockSpec(memory_space=pltpu.VMEM)] * 3,
         scratch_shapes=[
             pltpu.VMEM((depth, features.shape[0]), jnp.bfloat16),
             pltpu.VMEM((n, rows, width), jnp.bfloat16),
             pltpu.VMEM((n, rows, width), jnp.bfloat16),
             pltpu.VMEM((n, rows, width), jnp.bfloat16),
-            pltpu.VMEM((2, 2, half + 1, rows, width // 2), jnp.float32),
+            pltpu.VMEM((2, 2, half + 1, rows, width // 2), jnp.int16),
+            pltpu.VMEM((2, 2, half + 1, 1, width // 2), jnp.float32),
             pltpu.VMEM((8, width), jnp.float32),
+            pltpu.VMEM(scores.shape, jnp.float32),
             dma((n,)),
             dma((n,)),
             dma((2, 2, half)),
             dma((2, 2, half)),
+            dma((2, 2, half)),
+            dma((2, 2, half)),
+            dma((experts,)),
+            dma((experts,)),
             dma,
             dma,
         ],
@@ -209,7 +600,7 @@
             bytes_accessed=4 * depth * width,
             transcendentals=0,
         ),
-    )(features, dgu)
+    )(features, dgu, scores, targets)
 
 
 def shifted(block, axis, distance):
@@ -246,56 +637,24 @@
     groups = lax.axis_size("expert")
     dp_count = lax.axis_size("dp")
     experts = groups * local_experts
+    n = dp_count // 2
     row_count = token_count * choice_count
     capacity = 2 * row_count // experts
-    row_expert = routes.reshape(row_count)
-    onehot = (row_expert[:, None] == jnp.arange(experts, dtype=jnp.int32)[None, :]).astype(
-        jnp.int32
-    )
-    earlier = jnp.cumsum(onehot, axis=0) - onehot
-    row_slot = jnp.sum(earlier * onehot, axis=1)
-    target = jnp.arange(experts * capacity, dtype=jnp.int32)
-    select = (
-        (row_expert[None, :] == target[:, None] // capacity)
-        & (row_slot[None, :] == target[:, None] % capacity)
-    ).astype(jnp.bfloat16)
-    row_tokens = jnp.repeat(tokens, choice_count, axis=0)
-    row_grads = jnp.repeat(out_grad, choice_count, axis=0)
-    payload = jnp.concatenate(
-        [row_tokens, row_grads, gate_up.reshape(row_count, 2 * hidden)], axis=1
-    )
-    packed = jnp.dot(select, payload, preferred_element_type=jnp.float32).astype(jnp.bfloat16)
-    packed = packed.reshape(experts, capacity, payload.shape[1])
-    weight_sent = jnp.dot(select, route_weight, preferred_element_type=jnp.float32)
-    weight_sent = weight_sent.reshape(experts, capacity).astype(jnp.bfloat16)
-    arrived, arrived_weight = (
-        lax.all_to_all(packed, "expert", split_axis=0, concat_axis=1, tiled=True),
-        lax.all_to_all(weight_sent, "expert", split_axis=0, concat_axis=1, tiled=True),
-    )
-    features = arrived[:, :, :model_width]
-    cotangent = arrived[:, :, model_width : 2 * model_width]
-    saved_gu = arrived[:, :, 2 * model_width :]
-    back_prod = jnp.einsum(
-        "lrd,lkd->lrk",
-        cotangent,
-        lax.all_gather(down_weight, "dp", axis=1, tiled=True),
-        preferred_element_type=jnp.float32,
-    )
-    gate_pre = saved_gu[:, :, :hidden].astype(jnp.float32)
-    up_part = saved_gu[:, :, hidden:].astype(jnp.float32)
-    sigmoid_gate = jax.nn.sigmoid(gate_pre)
-    activation = gate_pre * sigmoid_gate * up_part
-    scores = jnp.sum(activation * back_prod, axis=2)
-    scaled = arrived_weight.astype(jnp.float32)[:, :, None] * back_prod
-    grad_gate = scaled * up_part * sigmoid_gate * (1.0 + gate_pre * (1.0 - sigmoid_gate))
-    grad_up = scaled * gate_pre * sigmoid_gate
-    grad_joined = jnp.concatenate([grad_gate, grad_up], axis=2).astype(jnp.bfloat16)
-    row_block, below_rows = sum_over_slabs(features[0], grad_joined[0], dp_count // 2)
-    returned = lax.all_to_all(scores, "expert", split_axis=1, concat_axis=0, tiled=True)
-    flat_scores = returned.reshape(experts * capacity)
-    router_grad = jnp.take(flat_scores, row_expert * capacity + row_slot).reshape(
-        token_count, choice_count
-    )
+    features, grad_joined, scores, targets = rows_to_experts(
+        tokens,
+        out_grad,
+        gate_up.reshape(row_count, 2 * hidden),
+        route_weight,
+        routes,
+        down_weight[0],
+        n,
+        experts,
+        capacity,
+    )
+    row_block, below_rows, router_row = sum_over_slabs(
+        features, grad_joined, scores, targets, n, experts
+    )
+    router_grad = router_row.reshape(token_count, choice_count)
     flat_size = model_width * 2 * hidden
     even_size = flat_size // dp_count
     margin_size = bucket_cap - even_size

time: 222 us -> 153 us (0.69)
  waiting for transfers between devices: 58.3 us -> 0.01 us
  Pallas kernels: 90.2 us -> 124 us
  starting transfers between devices: 22.2 us -> 4.01 us
  between operations: 16.9 us -> 3.38 us
  matrix products: 9.51 us -> 0 us
  other arithmetic: 14.2 us -> 11.1 us
    all_to_all x3 -> x0, waiting for transfers between devices: 39 us -> none  [the longest x1 33.4 us: shards(): lax.all_to_all(packed, 'expert', split_axis=0, concat_axis=1, tiled=True)]
    pallas_call x1 -> x2, Pallas kernels: 90.2 us -> 124 us  [the longest x1 67.1 us: rows_to_experts(): pl.pallas_call(functools.partial(send_kernel, n, experts), out_shape=(jax...]
    all_to_all x3 -> x0, starting transfers between devices: 18.7 us -> none  [the longest x1 7.58 us: shards(): lax.all_to_all(weight_sent, 'expert', split_axis=0, concat_axis=1, tiled=...]
    all_gather x1 -> x0, waiting for transfers between devices: 18.7 us -> none  [shards(): lax.all_gather(down_weight, 'dp', axis=1, tiled=True)]
    dot_general x3 -> x0, matrix products: 9.51 us -> none  [the longest x1 4.28 us: shards(): jnp.dot(select, payload, preferred_element_type=jnp.float32)]
    unnamed x18 -> x20, local copies, waits for them, and re-layouts: 2.35 us -> 6.88 us
  transfers between devices with their start and end apart: 5 -> 1, of which waited for: 4 -> 0; matrix products, arithmetic and copies ran while one was open for 8% -> 2% of each run, Pallas kernels for 0% -> 0%
where the time goes in v2:
time: 153 us; the launch traced here: 152 us
  Pallas kernels  124 us (81%)
  other arithmetic  11.1 us (7%)
  local copies, waits for them, and re-layouts  9.62 us (6%)
  starting transfers between devices  4.01 us (3%)
  between operations  3.38 us (2%)
    pallas_call x1, Pallas kernels, rows_to_experts(): pl.pallas_call(functools.partial(send_kernel, n, experts), out_shape=(jax...  67.1 us
    pallas_call x1, Pallas kernels, sum_over_slabs(): pl.pallas_call(functools.partial(sum_kernel, n, experts), out_shape=(jax....  57.3 us
    unnamed x20, local copies, waits for them, and re-layouts  6.88 us
    convert_element_type x1, other arithmetic, shards(): weight_half = new_master.astype(jnp.bfloat16)  5.96 us
    ppermute x1, starting transfers between devices, shifted(): return lax.ppermute(block, axis, route)  4.01 us
  transfers between devices with their start and end apart: 1, of which 0 were waited for; matrix products, arithmetic and copies ran while one was open for 2% of the time, Pallas kernels for 0%

profile of v2, /device:TPU:1, one launch (start us, length us, event | category | flops | bytes accessed | tf_op | source)
XLA Modules:
  0.0 152.4 jit_solution(14257876846493849092)
XLA Ops:
  0.6 1.3 fusion.12
  3.9 0.8 copy.15.weight_ref
  4.7 0.0 copy-start
  4.7 1.1 copy-done
  5.8 0.0 copy-start.1
  5.8 1.1 copy-done.1
  6.9 0.0 copy-start.2
  6.9 1.0 copy-done.2
  7.9 0.0 copy-start.3
  7.9 0.9 copy-done.3
  8.8 0.0 copy-start.4
  8.8 0.7 copy-done.4
  9.4 67.1 %shard_map.137 = (bf16[256,2560]{1,0:T(8,128)(2,1)S(1)}, bf16[256,1536]{1,0:T(8,128)(2,1)S(1)}, f32[256,128]{1,0:T(8,128)S(1)}, s32[1,128]{1,0:T(1,128)S(1)}) custom-call(bf16[128,2560]{1,0:T(8,128)(2,1)S(1)} %copy-done, bf16[128,2560]{1,0:T(8,128)(2,1)S(1)} %copy-done.1, bf16[128,1536]{1,0:T(8,128)(2,1)S(1)} %bitcast.45, ...), custom_call_target="tpu_custom_call" | custom-call | flops 1283457024 | bytes 4325376 | tf_op jit(solution)/shard_map/pallas_call | solution.py:301
  76.5 57.3 %shard_map.138 = (f32[80,1536]{1,0:T(8,128)S(1)}, f32[8,1536]{1,0:T(8,128)S(1)}, f32[1,128]{1,0:T(1,128)S(1)}) custom-call(bf16[256,2560]{1,0:T(8,128)(2,1)S(1)} %get-tuple-element.12.feat_ref, bf16[256,1536]{1,0:T(8,128)(2,1)S(1)} %get-tuple-element.13.dgu_ref, f32[256,128]{1,0:T(8,128)S(1)} %get-tuple-element.14.score_ref, ...), custom_call_target="tpu_custom_call" | custom-call | flops 2013265920 | bytes 15728640 | tf_op jit(solution)/shard_map/pallas_call | solution.py:566
  133.8 0.0 copy-start.5
  133.8 0.0 copy-start.6
  133.8 0.0 copy-start.7
  133.8 0.5 copy.17
  134.3 0.1 copy.16
  134.5 0.4 reshape.82
  134.8 0.0 copy-done.5
  134.9 0.1 copy-done.6
  135.0 0.2 copy-done.7
  135.1 6.0 %fusion.9 = (bf16[1,126720]{1,0:T(2,128)(2,1)S(1)}, f32[1,126720]{1,0:T(1,128)}, f32[1,126720]{1,0:T(1,128)S(1)}) fusion(f32[1,1,126720]{2,1,0:T(1,128)S(1)} %copy-done.5, f32[1,1,126720]{2,1,0:T(1,128)S(1)} %copy-done.6, f32[1,1,126720]{2,1,0:T(1,128)S(1)} %copy-done.7, s32[]{:T(128)S(6)} %sub.12, f32[1,130560]{1,0:T(1,128)S(1)} %reshape.82, ...), kind=kLoop, calls=%fused_computation.19 | loop fusion | flops 2661120 | bytes 3801608 | tf_op jit(solution)/shard_map/convert_element_type | solution.py:688
  141.1 4.0 %collective-permute-start = (bf16[1,3840]{1,0:T(2,128)(2,1)S(1)}, bf16[1,3840]{1,0:T(2,128)(2,1)S(1)}, u32[]{:S(2)}, u32[]{:S(2)}) collective-permute-start(bf16[1,3840]{1,0:T(2,128)(2,1)S(1)} %slice.9), channel_id=1, source_target_pairs={{16,0},{32,16},{48,32},{64,48},{80,64},{96,80},{112,96},{128,112},... | collective-permute-start | bytes 23048 | tf_op jit(solution)/shard_map/ppermute | solution.py:609
  145.1 2.8 %select_bitcast_fusion = (f32[1,1,126720]{2,1,0:T(1,128)}, f32[1,1,126720]{2,1,0:T(1,128)}) fusion(s32[]{:T(128)S(6)} %sub.12, f32[1,126720]{1,0:T(1,128)S(1)} %get-tuple-element.21, f32[1,1,126720]{2,1,0:T(1,128)S(1)} %copy-done.5, f32[1,1,126720]{2,1,0:T(1,128)S(1)} %copy-done.6), kind=kLoop, calls=%fused_computation.13 | loop fusion | flops 1267200 | bytes 2534404 | tf_op jit(solution)/shard_map/broadcast_in_dim | solution.py:701
  148.6 0.0 collective-permute-done
  148.6 2.4 %fusion.8 = bf16[122880]{0:T(1024)(128)(2,1)S(1)} fusion(s32[]{:T(128)S(6)} %select_n.36, bf16[1,3840]{1,0:T(2,128)(2,1)S(1)} %collective-permute-done, bf16[1,126720]{1,0:T(2,128)(2,1)S(1)} %get-tuple-element.19, s32[]{:T(128)S(6)} %select_n.35), kind=kLoop, calls=%fused_computation.18 | loop fusion | flops 491520 | bytes 499208 | tf_op jit(solution)/shard_map/add | solution.py:697
  150.9 1.0 reshape.79
  151.9 0.5 copy.19
  (4 shorter events, 0.1 us)
Async XLA Ops:
  4.7 1.1 copy-start
  5.8 1.1 copy-start.1
  6.9 1.0 copy-start.2
  7.9 0.9 copy-start.3
  8.8 0.7 copy-start.4
  133.8 1.1 copy-start.5
  133.8 1.2 copy-start.6
  133.8 1.3 copy-start.7
  141.1 7.5 %collective-permute-start = (bf16[1,3840]{1,0:T(2,128)(2,1)S(1)}, bf16[1,3840]{1,0:T(2,128)(2,1)S(1)}, u32[]{:S(2)}, u32[]{:S(2)}) collective-permute-start(bf16[1,3840]{1,0:T(2,128)(2,1)S(1)} %slice.9), channel_id=1, source_target_pairs={{16,0},{32,16},{48,32},{64,48},{80,64},{96,80},{112,96},{128,112},... | collective-permute-start | bytes 23048 | tf_op jit(solution)/shard_map/ppermute | solution.py:609

commit v3 on v1

v3 whole, which is shorter than its diff:
```python
import functools

import jax
import jax.numpy as jnp
from jax import lax
from jax.experimental import pallas as pl
from jax.experimental.pallas import tpu as pltpu
from jax.sharding import PartitionSpec as P

beta_one = 0.9
beta_two = 0.95
learn_rate = 0.001
decay_rate = 0.1
adam_eps = 1e-08
adam_step = 20.0

MESH = pl.DeviceIdType.MESH


ONE_CUTS = 3
TWO_CUTS = 2


def distance(i, side):
    dx, dy = i // side, i % side
    return min(dx, 4 - dx) + min(dy, side - dy), -min(dx, 4 - dx), -min(i, 16 - i)


def grad_kernel(
    n,
    experts,
    tok_ref,
    grad_ref,
    saved_ref,
    weight_ref,
    route_ref,
    down_ref,
    out_ref,
    tail_ref,
    router_ref,
    tok_in,
    grad_in,
    saved_in,
    down_in,
    pack_one,
    pack_two,
    rows_in,
    feats,
    down_wide,
    down_sib,
    down_all,
    dgu,
    score,
    score_in,
    feat_t,
    own,
    give,
    sib,
    work,
    scale,
    tail_in,
    load_sem,
    one_send,
    one_recv,
    two_send,
    two_recv,
    ring_send,
    ring_recv,
    pass_send,
    pass_recv,
    first_send,
    first_recv,
    score_send,
    score_recv,
    sib_send,
    sib_recv,
    sum_send,
    sum_recv,
    scale_send,
    scale_recv,
    tail_send,
    tail_recv,
):
    half = n // 2
    count, depth = tok_ref.shape
    hidden = saved_ref.shape[1] // 2
    slots = rows_in.shape[0] // experts
    share = down_ref.shape[0]
    part = depth // 4
    rows, width = out_ref.shape
    cols = width // 2
    side = 4 if experts % 4 == 0 else experts
    dp = lax.axis_index("dp")
    me = lax.axis_index("expert")
    z, c = dp // 2, dp % 2
    other = (z * 2 + 1 - c, me)
    ahead = (lax.rem(z + 1, n) * 2 + c, me)
    behind = (lax.rem(z + n - 1, n) * 2 + c, me)
    upper = (lax.rem(dp + 1, 2 * n), me)
    lower = (lax.rem(dp + 2 * n - 1, 2 * n), me)
    every = ((0, 0), (1, 1), (0, 1), (1, 0))

    def peer_at(dx, dy):
        x = lax.rem(me // side + dx + 4 * side, experts // side)
        return x * side + lax.rem(me % side + dy + 4 * side, side)

    def peer(i):
        return peer_at(i // side, i % side)

    far = sorted(range(1, experts), key=lambda i: distance(i, side), reverse=True)

    def remote(source, target, send, recv, device):
        return pltpu.make_async_remote_copy(
            src_ref=source,
            dst_ref=target,
            send_sem=send,
            recv_sem=recv,
            device_id=device,
            device_id_type=MESH,
        )

    barrier = pltpu.get_barrier_semaphore()
    for device in (other, ahead, behind, upper, lower):
        pl.semaphore_signal(barrier, inc=1, device_id=device, device_id_type=MESH)

    def greet(i, _):
        pl.semaphore_signal(barrier, inc=1, device_id=(dp, peer(i)), device_id_type=MESH)
        return 0

    lax.fori_loop(1, experts, greet, 0)

    loads = [
        pltpu.make_async_copy(source, target, load_sem.at[i])
        for i, (source, target) in enumerate(
            ((down_ref, down_in), (grad_ref, grad_in), (saved_ref, saved_in), (tok_ref, tok_in))
        )
    ]
    for load in loads:
        load.start()

    first = remote(
        down_wide.at[:, pl.ds(pl.multiple_of((1 - c) * 2 * part, 128), 2 * part)],
        down_sib,
        first_send,
        first_recv,
        other,
    )

    def place(idx):
        return pl.ds(pl.multiple_of(lax.rem(idx + n, n) * 2 * share, 16), 2 * share)

    def down_copy(d, u, s):
        block = down_all.at[c, place(z - s if d == 0 else z + s), pl.ds(u * part, part)]
        return remote(
            block, block, ring_send.at[d, u, s], ring_recv.at[d, u, s], (ahead, behind)[d]
        )

    def pass_copy(r, half_at):
        block = down_all.at[half_at, place(z + r)]
        return remote(block, block, pass_send.at[r], pass_recv.at[r], other)

    route = route_ref[...]
    expert_id = lax.broadcasted_iota(jnp.int32, (experts, count), 0)
    onehot = jnp.where(route == expert_id, 1.0, 0.0)
    before = lax.broadcasted_iota(jnp.int32, (count, count), 0)
    after = lax.broadcasted_iota(jnp.int32, (count, count), 1)
    ahead_of = jnp.where(before < after, 1.0, 0.0).astype(jnp.bfloat16)
    earlier = jnp.dot(onehot.astype(jnp.bfloat16), ahead_of, preferred_element_type=jnp.float32)
    slot = jnp.sum(earlier * onehot, axis=0, keepdims=True).astype(jnp.int32)
    target = route * slots + slot
    slot_id = lax.broadcasted_iota(jnp.int32, (experts * slots, count), 0)
    chosen = jnp.where(slot_id == target, 1.0, 0.0)
    select = chosen.astype(jnp.bfloat16)
    slot_weight = jnp.sum(chosen * weight_ref[...].astype(jnp.float32), axis=1, keepdims=True)

    def pack(into, cuts, p, sources):
        size = into.shape[1] // cuts
        left = 0
        for source in sources:
            low, high = max(p * size, left), min((p + 1) * size, left + source.shape[1])
            if low < high:
                into[:, pl.ds(low, high - low)] = jnp.dot(
                    select,
                    source[:, pl.ds(low - left, high - low)],
                    preferred_element_type=jnp.float32,
                ).astype(jnp.bfloat16)
            left += source.shape[1]

    def block(e):
        return pl.ds(pl.multiple_of(e * slots, 16), slots)

    def one_copy(i, p):
        size = pack_one.shape[1] // ONE_CUTS
        at = pl.ds(pl.multiple_of(p * size, 128), size)
        return remote(
            pack_one.at[block(peer(i)), at],
            rows_in.at[block(me), at],
            one_send.at[i, p],
            one_recv.at[i, p],
            (dp, peer(i)),
        )

    def two_copy(i, p):
        size = pack_two.shape[1] // TWO_CUTS
        at = pl.ds(pl.multiple_of(p * size, 128), size)
        return remote(
            pack_two.at[block(peer(i)), at],
            feats.at[block(me), at],
            two_send.at[i, p],
            two_recv.at[i, p],
            (dp, peer(i)),
        )

    loads[0].wait()
    down_wide[...] = down_in[...].astype(jnp.float32)
    pl.semaphore_wait(barrier, experts + 4)
    first.start()
    pack_one[:, pl.ds(depth + 2 * hidden, 128)] = jnp.broadcast_to(
        slot_weight, (experts * slots, 128)
    ).astype(jnp.bfloat16)
    loads[1].wait()
    loads[2].wait()
    pack(pack_one, ONE_CUTS, 0, (grad_in, saved_in))
    for i in far:
        one_copy(i, 0).start()
    first.wait()
    mine = down_wide[:, pl.ds(pl.multiple_of(c * 2 * part, 128), 2 * part)]
    theirs = down_sib[...]
    top, low = jnp.where(c == 0, mine, theirs), jnp.where(c == 0, theirs, mine)
    down_all[c, place(z), :] = jnp.concatenate([top, low], axis=0).astype(jnp.bfloat16)
    for d, u in every:
        down_copy(d, u, 0).start()
    pass_copy(0, c).start()
    for p in range(1, ONE_CUTS):
        pack(pack_one, ONE_CUTS, p, (grad_in, saved_in))
        for i in far:
            one_copy(i, p).start()
    loads[3].wait()
    for p in range(TWO_CUTS):
        pack(pack_two, TWO_CUTS, p, (tok_in,))
        for i in far:
            two_copy(i, p).start()
    rows_in[block(me), :] = pack_one[block(me), :]
    feats[block(me), :] = pack_two[block(me), :]

    def forward(s, _):
        for d, u in every:
            down_copy(d, u, s - 1).wait_recv()
            if d == u:
                down_copy(d, u, s).start()
            else:

                @pl.when(s < half - 1)
                def _():
                    down_copy(d, u, s).start()

        pass_copy(n - s, c).start()
        pass_copy(s, c).start()
        return 0

    lax.fori_loop(1, half, forward, 0)
    for u in range(2):
        down_copy(u, u, half - 1).wait_recv()
    pass_copy(half, c).start()

    def land_one(i, _):
        for p in range(ONE_CUTS):
            one_copy(i, p).wait_recv()
        return 0

    lax.fori_loop(1, experts, land_one, 0)

    def land_pass(r, _):
        pass_copy(r, 1 - c).wait_recv()
        return 0

    lax.fori_loop(0, n, land_pass, 0)

    tile = 256
    weight = rows_in[:, pl.ds(depth + 2 * hidden, 128)].astype(jnp.float32)[:, :1]
    total = jnp.zeros((experts * slots, 1), jnp.float32)
    for j in range(hidden // tile):
        back = sum(
            lax.dot_general(
                rows_in[:, pl.ds(h * 2 * part, 2 * part)],
                down_all[h, pl.ds(j * tile, tile), :],
                (((1,), (1,)), ((), ())),
                preferred_element_type=jnp.float32,
            )
            for h in range(2)
        )
        gate = rows_in[:, pl.ds(depth + j * tile, tile)].astype(jnp.float32)
        up = rows_in[:, pl.ds(depth + hidden + j * tile, tile)].astype(jnp.float32)
        sig = 1.0 / (1.0 + jnp.exp(-gate))
        silu = gate * sig
        total = total + jnp.sum(silu * up * back, axis=1, keepdims=True)
        scaled = weight * back
        dgu[:, pl.ds(j * tile, tile)] = (
            scaled * up * sig * (1.0 + gate * (1.0 - sig))
        ).astype(jnp.bfloat16)
        dgu[:, pl.ds(hidden + j * tile, tile)] = (scaled * silu).astype(jnp.bfloat16)
    score[...] = jnp.broadcast_to(total, score.shape)

    def score_copy(i):
        return remote(
            score.at[pl.ds(pl.multiple_of(peer(i) * slots, 8), slots)],
            score_in.at[pl.ds(pl.multiple_of(me * slots, 8), slots)],
            score_send.at[i],
            score_recv.at[i],
            (dp, peer(i)),
        )

    def land_two(i, _):
        for p in range(TWO_CUTS):
            two_copy(i, p).wait_recv()
        return 0

    lax.fori_loop(1, experts, land_two, 0)
    for i in range(depth // 256):
        feat_t[pl.ds(i * 256, 256), :] = feats[:, pl.ds(i * 256, 256)].T

    def sib_copy(r):
        return remote(give.at[r], sib.at[r], sib_send.at[r], sib_recv.at[r], other)

    def ring_copy(d, u, s):
        return [
            remote(
                buffer.at[d, u, s],
                buffer.at[d, u, s + 1],
                send.at[d, u, s],
                recv.at[d, u, s],
                (ahead, behind)[d],
            )
            for buffer, send, recv in (
                (work, sum_send, sum_recv),
                (scale, scale_send, scale_recv),
            )
        ]

    def produce(places):
        pieces = []
        for r in places:
            owner = lax.rem(z + r, n)
            for core in (c, 1 - c):
                start = pl.multiple_of((owner * 2 + core) * rows, 16)
                pieces.append(feat_t[pl.ds(start, rows), :])
        lhs = jnp.concatenate(pieces, axis=0)
        for j in range(width // 256):
            at = pl.ds(j * 256, 256)
            prod = jnp.dot(lhs, dgu[:, at], preferred_element_type=jnp.float32)
            prod = prod.astype(jnp.bfloat16)
            for i, r in enumerate(places):
                own[r, :, at] = prod[2 * i * rows : (2 * i + 1) * rows]
                give[r, :, at] = prod[(2 * i + 1) * rows : (2 * i + 2) * rows]

    def chip_sum(r, u):
        at = pl.ds(u * cols, cols)
        return own[r, :, at].astype(jnp.float32) + sib[r, :, at].astype(jnp.float32)

    def decoded(d, u, s):
        return work[d, u, s].astype(jnp.int32).astype(jnp.float32) * scale[d, u, s]

    def step(s, streams, fresh):
        k = half - s
        for d, u in streams:
            r = k if d == 0 else n - k
            value = chip_sum(r, u)
            if (d, u) not in fresh:
                for copy in ring_copy(d, u, s - 1):
                    copy.wait_recv()
                value = value + decoded(d, u, s)
            most = jnp.maximum(jnp.max(jnp.abs(value), axis=0, keepdims=True), 1e-30)
            scale[d, u, s] = most * (1.0 / 32767.0)
            coded = jnp.round(value * (32767.0 / most))
            work[d, u, s] = coded.astype(jnp.int32).astype(jnp.int16)
            for copy in ring_copy(d, u, s):
                copy.start()

    produce([half])
    sib_copy(half).start()
    produce([half - 1, half + 1])
    sib_copy(half - 1).start()
    sib_copy(half + 1).start()
    sib_copy(half).wait_recv()
    step(0, every[:2], every[:2])

    def send_score(i, _):
        score_copy(i).start()
        return 0

    lax.fori_loop(1, experts, send_score, 0)
    mine_at = pl.ds(pl.multiple_of(me * slots, 8), slots)
    score_in[mine_at, :] = score[mine_at, :]

    def body(s, _):
        k = half - s
        sib_copy(k).wait_recv()
        sib_copy(n - k).wait_recv()

        @pl.when(s == 1)
        def _():
            step(s, every, every[2:])

        @pl.when(s > 1)
        def _():
            step(s, every, ())

        @pl.when(k > 1)
        def _():
            produce([k - 1, n - k + 1])
            sib_copy(k - 1).start()
            sib_copy(n - k + 1).start()

        return 0

    lax.fori_loop(1, half, body, 0)
    produce([0])
    sib_copy(0).start()

    def land_score(i, _):
        score_copy(i).wait()
        return 0

    lax.fori_loop(1, experts, land_score, 0)
    router_ref[...] = jnp.sum(chosen * score_in[...], axis=0, keepdims=True)

    def drain_one(i, _):
        for p in range(ONE_CUTS):
            one_copy(i, p).wait_send()
        for p in range(TWO_CUTS):
            two_copy(i, p).wait_send()
        return 0

    lax.fori_loop(1, experts, drain_one, 0)
    def drain_pass(r, _):
        pass_copy(r, c).wait_send()
        return 0

    lax.fori_loop(0, n, drain_pass, 0)

    def drain_down(s, _):
        for d, u in every:
            down_copy(d, u, s).wait_send()
        return 0

    lax.fori_loop(0, half - 1, drain_down, 0)
    for u in range(2):
        down_copy(u, u, half - 1).wait_send()

    def drain_sum(s, _):
        for d, u in every:
            for copy in ring_copy(d, u, s):
                copy.wait_send()
        return 0

    for d, u in every[:2]:
        for copy in ring_copy(d, u, 0):
            copy.wait_send()
    lax.fori_loop(1, half - 1, drain_sum, 0)
    sib_copy(0).wait_recv()
    for u in range(2):
        for d in range(2):
            for copy in ring_copy(d, u, half - 1):
                copy.wait_recv()
        out_ref[:, pl.ds(u * cols, cols)] = chip_sum(0, u) + (
            decoded(0, u, half) + decoded(1, u, half)
        )
    last = remote(out_ref.at[pl.ds(rows - 8, 8)], tail_in, tail_send, tail_recv, upper)
    last.start()

    def drain_sib(r, _):
        sib_copy(r).wait_send()
        return 0

    lax.fori_loop(0, n, drain_sib, 0)
    drain_sum(half - 1, 0)
    last.wait()
    tail_ref[...] = tail_in[...]


def weight_gradient(tokens, out_grad, saved, weight, routes, down, n, experts, slots):
    count, depth = tokens.shape
    hidden = saved.shape[1] // 2
    width = 2 * hidden
    total = experts * slots
    rows = depth // (2 * n)
    half = n // 2
    wide = depth + width + 128
    dma = pltpu.SemaphoreType.DMA
    bf16, f32 = jnp.bfloat16, jnp.float32
    anywhere = pl.BlockSpec(memory_space=pl.ANY)
    inside = pl.BlockSpec(memory_space=pltpu.VMEM)
    return pl.pallas_call(
        functools.partial(grad_kernel, n, experts),
        out_shape=(
            jax.ShapeDtypeStruct((rows, width), f32),
            jax.ShapeDtypeStruct((8, width), f32),
            jax.ShapeDtypeStruct((1, count), f32),
        ),
        in_specs=[anywhere, anywhere, anywhere, inside, inside, anywhere],
        out_specs=[inside] * 3,
        scratch_shapes=[
            pltpu.VMEM(tokens.shape, bf16),
            pltpu.VMEM(out_grad.shape, bf16),
            pltpu.VMEM(saved.shape, bf16),
            pltpu.VMEM(down.shape, bf16),
            pltpu.VMEM((total, wide), bf16),
            pltpu.VMEM((total, depth), bf16),
            pltpu.VMEM((total, wide), bf16),
            pltpu.VMEM((total, depth), bf16),
            pltpu.VMEM(down.shape, f32),
            pltpu.VMEM((down.shape[0], depth // 2), f32),
            pltpu.VMEM((2, hidden, depth // 2), bf16),
            pltpu.VMEM((total, width), bf16),
            pltpu.VMEM((total, count), f32),
            pltpu.VMEM((total, count), f32),
            pltpu.VMEM((depth, total), bf16),
            pltpu.VMEM((n, rows, width), bf16),
            pltpu.VMEM((n, rows, width), bf16),
            pltpu.VMEM((n, rows, width), bf16),
            pltpu.VMEM((2, 2, half + 1, rows, width // 2), jnp.int16),
            pltpu.VMEM((2, 2, half + 1, 1, width // 2), f32),
            pltpu.VMEM((8, width), f32),
            dma((4,)),
            dma((experts, ONE_CUTS)),
            dma((experts, ONE_CUTS)),
            dma((experts, TWO_CUTS)),
            dma((experts, TWO_CUTS)),
            dma((2, 2, half)),
            dma((2, 2, half)),
            dma((n,)),
            dma((n,)),
            dma,
            dma,
            dma((experts,)),
            dma((experts,)),
            dma((n,)),
            dma((n,)),
            dma((2, 2, half)),
            dma((2, 2, half)),
            dma((2, 2, half)),
            dma((2, 2, half)),
            dma,
            dma,
        ],
        compiler_params=pltpu.CompilerParams(
            collective_id=0, has_side_effects=True, vmem_limit_bytes=60 * 2**20
        ),
        cost_estimate=pl.CostEstimate(
            flops=2 * total * (depth * hidden + depth * width + count * wide),
            bytes_accessed=2 * count * wide,
            transcendentals=total * hidden,
        ),
    )(
        tokens,
        out_grad,
        saved,
        weight.reshape(1, count),
        routes.reshape(1, count),
        down,
    )


def shifted(block, axis, distance):
    devices = range(lax.axis_size(axis))
    route = [(i - distance, i) for i in devices if i - distance in devices]
    return lax.ppermute(block, axis, route)


def cut_window(source, from_index, window_len):
    return lax.dynamic_slice_in_dim(source, from_index, window_len, 1)


def zero_cols(row_count, col_count, kind):
    return jnp.zeros((row_count, col_count), kind)


def shards(
    tokens,
    out_grad,
    gate_up,
    route_weight,
    routes,
    down_weight,
    master,
    moment_one,
    moment_two,
    offsets,
):
    token_count, model_width = tokens.shape
    choice_count = routes.shape[1]
    hidden = gate_up.shape[2] // 2
    local_experts = master.shape[0]
    bucket_cap = master.shape[2]
    groups = lax.axis_size("expert")
    dp_count = lax.axis_size("dp")
    experts = groups * local_experts
    n = dp_count // 2
    row_count = token_count * choice_count
    capacity = 2 * row_count // experts
    row_block, below_rows, router_row = weight_gradient(
        tokens,
        out_grad,
        gate_up.reshape(row_count, 2 * hidden),
        route_weight,
        routes,
        down_weight[0],
        n,
        experts,
        capacity,
    )
    router_grad = router_row.reshape(token_count, choice_count)
    flat_size = model_width * 2 * hidden
    even_size = flat_size // dp_count
    margin_size = bucket_cap - even_size
    position = lax.axis_index("dp")
    start_at = offsets[position]
    finish = offsets[position + 1]
    bucket_len = finish - start_at
    lead_shift = start_at - position * even_size
    tail_shift = finish - (position + 1) * even_size
    slot_ids = jnp.arange(bucket_cap, dtype=jnp.int32)
    in_bucket = slot_ids < bucket_len
    row_sum = row_block.reshape(1, even_size)
    from_below = below_rows.reshape(1, -1)[:, -margin_size:]
    extended = jnp.concatenate(
        [from_below, row_sum, zero_cols(local_experts, margin_size, jnp.float32)], axis=1
    )
    bucket_grad = cut_window(extended, lead_shift + margin_size, bucket_cap)
    bucket_grad = jnp.where(in_bucket[None, :], bucket_grad, 0.0)
    old_master = master[:, 0, :]
    moment_new = beta_one * moment_one[:, 0, :] + (1.0 - beta_one) * bucket_grad
    square_new = beta_two * moment_two[:, 0, :] + (1.0 - beta_two) * bucket_grad * bucket_grad
    update = (
        moment_new
        / (1.0 - beta_one**adam_step)
        / (jnp.sqrt(square_new / (1.0 - beta_two**adam_step)) + adam_eps)
    )
    master_new = old_master - learn_rate * (update + decay_rate * old_master)
    new_master = jnp.where(in_bucket[None, :], master_new, 0.0)
    new_moment_one = jnp.where(in_bucket[None, :], moment_new, 0.0)
    new_moment_two = jnp.where(in_bucket[None, :], square_new, 0.0)
    weight_half = new_master.astype(jnp.bfloat16)
    head_part = weight_half[:, :margin_size]
    from_above = shifted(head_part, "dp", -1)
    from_own = cut_window(weight_half, -lead_shift, even_size)
    from_next = cut_window(
        jnp.concatenate([zero_cols(local_experts, even_size, jnp.bfloat16), from_above], axis=1),
        -tail_shift,
        even_size,
    )
    new_weight = (from_own + from_next).reshape(local_experts, model_width // dp_count, 2 * hidden)
    return (
        new_master[:, None, :],
        new_moment_one[:, None, :],
        new_moment_two[:, None, :],
        new_weight,
        router_grad,
    )


def solution(mesh):
    placed = (
        P(("dp", "expert"), None),
        P(("dp", "expert"), None),
        P(("dp", "expert"), None, None),
        P(("dp", "expert"), None),
        P(("dp", "expert"), None),
        P("expert", "dp", None),
        P("expert", "dp", None),
        P("expert", "dp", None),
        P("expert", "dp", None),
        P(),
    )
    return jax.shard_map(
        shards,
        mesh=mesh,
        in_specs=placed,
        out_specs=(
            P("expert", "dp", None),
            P("expert", "dp", None),
            P("expert", "dp", None),
            P("expert", "dp", None),
            P(("dp", "expert"), None),
        ),
        check_vma=False,
    )
```

time: 222 us -> 134 us (0.60)
  waiting for transfers between devices: 58.3 us -> 0.01 us
  Pallas kernels: 90.2 us -> 109 us
  starting transfers between devices: 22.2 us -> 3.97 us
  between operations: 16.9 us -> 3.38 us
  matrix products: 9.51 us -> 0 us
  local copies, waits for them, and re-layouts: 9.78 us -> 6.3 us
  other arithmetic: 14.2 us -> 11.1 us
    all_to_all x3 -> x0, waiting for transfers between devices: 39 us -> none  [the longest x1 33.4 us: shards(): lax.all_to_all(packed, 'expert', split_axis=0, concat_axis=1, tiled=True)]
    pallas_call x1, Pallas kernels: 90.2 us -> 109 us  [weight_gradient(): pl.pallas_call(functools.partial(grad_kernel, n, experts), out_shape=(jax...]
    all_to_all x3 -> x0, starting transfers between devices: 18.7 us -> none  [the longest x1 7.58 us: shards(): lax.all_to_all(weight_sent, 'expert', split_axis=0, concat_axis=1, tiled=...]
    all_gather x1 -> x0, waiting for transfers between devices: 18.7 us -> none  [shards(): lax.all_gather(down_weight, 'dp', axis=1, tiled=True)]
    dot_general x3 -> x0, matrix products: 9.51 us -> none  [the longest x1 4.28 us: shards(): jnp.dot(select, payload, preferred_element_type=jnp.float32)]
  transfers between devices with their start and end apart: 5 -> 1, of which waited for: 4 -> 0; matrix products, arithmetic and copies ran while one was open for 8% -> 2% of each run, Pallas kernels for 0% -> 0%
where the time goes in v3:
time: 134 us
  Pallas kernels  109 us (81%)
  other arithmetic  11.1 us (8%)
  local copies, waits for them, and re-layouts  6.3 us (5%)
  starting transfers between devices  3.97 us (3%)
  between operations  3.38 us (3%)
    pallas_call x1, Pallas kernels, weight_gradient(): pl.pallas_call(functools.partial(grad_kernel, n, experts), out_shape=(jax...  109 us
    convert_element_type x1, other arithmetic, shards(): weight_half = new_master.astype(jnp.bfloat16)  5.99 us
    unnamed x13, local copies, waits for them, and re-layouts  4.3 us
    ppermute x1, starting transfers between devices, shifted(): return lax.ppermute(block, axis, route)  3.97 us
    broadcast_in_dim x1, other arithmetic, shards(): new_moment_two[:, None, :]  2.78 us
  transfers between devices with their start and end apart: 1, of which 0 were waited for; matrix products, arithmetic and copies ran while one was open for 2% of the time, Pallas kernels for 0%

profile of v3, /device:TPU:1, one launch (start us, length us, event | category | flops | bytes accessed | tf_op | source)
XLA Modules:
  0.0 133.7 jit_solution(1936142872055006540)
XLA Ops:
  0.6 0.0 copy-start.3
  0.6 0.6 copy-done.3
  1.3 0.6 fusion.12
  3.9 0.4 reshape.86
  4.2 0.0 copy-start.2
  4.3 109.0 %shard_map.137 = (f32[80,1536]{1,0:T(8,128)}, f32[8,1536]{1,0:T(8,128)}, f32[1,128]{1,0:T(1,128)}) custom-call(bf16[128,2560]{1,0:T(8,128)(2,1)} %tok_ref.1, bf16[128,2560]{1,0:T(8,128)(2,1)} %grad_ref.1, bf16[128,1536]{1,0:T(8,128)(2,1)} %bitcast.49, bf16[1,128]{1,0:T(2,128)(2,1)} %bitcast.51, s32[1,128]{1,0:T(1,128)} %bitcast.52, bf16[24,2560]{1,0:T(8,128)(2,1)} %bitcast.50), custom_call_target="tpu_custom_call" | custom-call | flops 3296722944 | bytes 1081344 | tf_op jit(solution)/shard_map/pallas_call | solution.py:493
  113.2 0.9 copy.15
  114.1 0.0 copy-start
  114.1 0.0 copy-start.1
  114.1 1.6 %copy.16 = f32[1,1,80,1536]{3,1,2,0:T(1,128)S(1)} copy(f32[1,1,80,1536]{3,2,1,0:T(8,128)} %bitcast.46) | data formatting | bytes 983040
  115.8 0.0 copy-done.2
  115.8 0.0 copy-done
  115.8 0.0 copy-done.1
  115.8 6.0 %fusion.9 = (bf16[1,126720]{1,0:T(2,128)(2,1)S(1)}, f32[1,126720]{1,0:T(1,128)}, f32[1,126720]{1,0:T(1,128)S(1)}) fusion(f32[1,1,126720]{2,1,0:T(1,128)S(1)} %copy-done, f32[1,1,126720]{2,1,0:T(1,128)S(1)} %copy-done.1, f32[1,1,126720]{2,1,0:T(1,128)S(1)} %copy-done.2, s32[]{:T(128)S(6)} %sub.12, f32[1,130560]{1,0:T(1,128)S(1)} %reshape.86, ...), kind=kLoop, calls=%fused_computation.19 | loop fusion | flops 2661120 | bytes 3801608 | tf_op jit(solution)/shard_map/convert_element_type | solution.py:643
  121.8 4.0 %collective-permute-start = (bf16[1,3840]{1,0:T(2,128)(2,1)S(1)}, bf16[1,3840]{1,0:T(2,128)(2,1)S(1)}, u32[]{:S(2)}, u32[]{:S(2)}) collective-permute-start(bf16[1,3840]{1,0:T(2,128)(2,1)S(1)} %slice.9), channel_id=1, source_target_pairs={{16,0},{32,16},{48,32},{64,48},{80,64},{96,80},{112,96},{128,112},... | collective-permute-start | bytes 23048 | tf_op jit(solution)/shard_map/ppermute | solution.py:567
  125.8 2.8 %select_bitcast_fusion = (f32[1,1,126720]{2,1,0:T(1,128)}, f32[1,1,126720]{2,1,0:T(1,128)}) fusion(s32[]{:T(128)S(6)} %sub.12, f32[1,126720]{1,0:T(1,128)S(1)} %get-tuple-element.13, f32[1,1,126720]{2,1,0:T(1,128)S(1)} %copy-done, f32[1,1,126720]{2,1,0:T(1,128)S(1)} %copy-done.1), kind=kLoop, calls=%fused_computation.13 | loop fusion | flops 1267200 | bytes 2534404 | tf_op jit(solution)/shard_map/broadcast_in_dim | solution.py:656
  129.2 0.0 collective-permute-done
  129.2 2.3 %fusion.8 = bf16[122880]{0:T(1024)(128)(2,1)S(1)} fusion(s32[]{:T(128)S(6)} %select_n.36, bf16[1,3840]{1,0:T(2,128)(2,1)S(1)} %collective-permute-done, bf16[1,126720]{1,0:T(2,128)(2,1)S(1)} %get-tuple-element.11, s32[]{:T(128)S(6)} %select_n.35), kind=kLoop, calls=%fused_computation.18 | loop fusion | flops 491520 | bytes 499208 | tf_op jit(solution)/shard_map/add | solution.py:652
  131.6 1.0 reshape.83
  132.6 0.0 copy-start.4
  132.6 0.7 copy-done.4
  133.2 0.5 copy.18
  (4 shorter events, 0.1 us)
Async XLA Ops:
  0.6 0.7 copy-start.3
  4.2 111.5 %copy-start.2 = (f32[1,1,126720]{2,1,0:T(1,128)S(1)}, f32[1,1,126720]{2,1,0:T(1,128)}, u32[]{:S(2)}) copy-start(f32[1,1,126720]{2,1,0:T(1,128)} %param.16) | copy-start | bytes 1520644
  114.1 1.7 %copy-start = (f32[1,1,126720]{2,1,0:T(1,128)S(1)}, f32[1,1,126720]{2,1,0:T(1,128)}, u32[]{:S(2)}) copy-start(f32[1,1,126720]{2,1,0:T(1,128)} %param.18) | copy-start | bytes 1520644
  114.1 1.7 %copy-start.1 = (f32[1,1,126720]{2,1,0:T(1,128)S(1)}, f32[1,1,126720]{2,1,0:T(1,128)}, u32[]{:S(2)}) copy-start(f32[1,1,126720]{2,1,0:T(1,128)} %param.17) | copy-start | bytes 1520644
  121.8 7.4 %collective-permute-start = (bf16[1,3840]{1,0:T(2,128)(2,1)S(1)}, bf16[1,3840]{1,0:T(2,128)(2,1)S(1)}, u32[]{:S(2)}, u32[]{:S(2)}) collective-permute-start(bf16[1,3840]{1,0:T(2,128)(2,1)S(1)} %slice.9), channel_id=1, source_target_pairs={{16,0},{32,16},{48,32},{64,48},{80,64},{96,80},{112,96},{128,112},... | collective-permute-start | bytes 23048 | tf_op jit(solution)/shard_map/ppermute | solution.py:567
  132.6 0.7 copy-start.4

commit v4 on v3

--- a/solution.py
+++ b/solution.py
@@ -35,9 +35,13 @@
     weight_ref,
     route_ref,
     down_ref,
+    master_ref,
+    one_ref,
+    two_ref,
     out_ref,
     tail_ref,
     router_ref,
+    heads_ref,
     tok_in,
     grad_in,
     saved_in,
@@ -59,6 +63,7 @@
     work,
     scale,
     tail_in,
+    heads_in,
     load_sem,
     one_send,
     one_recv,
@@ -80,6 +85,8 @@
     scale_recv,
     tail_send,
     tail_recv,
+    head_send,
+    head_recv,
 ):
     half = n // 2
     count, depth = tok_ref.shape
@@ -209,6 +216,16 @@
             two_send.at[i, p],
             two_recv.at[i, p],
             (dp, peer(i)),
+        )
+
+    def head_copy(i):
+        source = (master_ref, one_ref, two_ref)[i]
+        return remote(
+            source.at[0, :, pl.ds(0, heads_in.shape[2])],
+            heads_in.at[i],
+            head_send.at[i],
+            head_recv.at[i],
+            lower,
         )
 
     loads[0].wait()
@@ -240,6 +257,8 @@
         pack(pack_two, TWO_CUTS, p, (tok_in,))
         for i in far:
             two_copy(i, p).start()
+    for i in range(3):
+        head_copy(i).start()
     rows_in[block(me), :] = pack_one[block(me), :]
     feats[block(me), :] = pack_two[block(me), :]
 
@@ -432,6 +451,10 @@
         return 0
 
     lax.fori_loop(1, experts, drain_one, 0)
+    for i in range(3):
+        head_copy(i).wait()
+    heads_ref[...] = heads_in[...]
+
     def drain_pass(r, _):
         pass_copy(r, c).wait_send()
         return 0
@@ -478,7 +501,9 @@
     tail_ref[...] = tail_in[...]
 
 
-def weight_gradient(tokens, out_grad, saved, weight, routes, down, n, experts, slots):
+def weight_gradient(
+    tokens, out_grad, saved, weight, routes, down, states, margin, n, experts, slots
+):
     count, depth = tokens.shape
     hidden = saved.shape[1] // 2
     width = 2 * hidden
@@ -496,9 +521,10 @@
             jax.ShapeDtypeStruct((rows, width), f32),
             jax.ShapeDtypeStruct((8, width), f32),
             jax.ShapeDtypeStruct((1, count), f32),
+            jax.ShapeDtypeStruct((3, 1, margin), f32),
         ),
-        in_specs=[anywhere, anywhere, anywhere, inside, inside, anywhere],
-        out_specs=[inside] * 3,
+        in_specs=[anywhere, anywhere, anywhere, inside, inside] + [anywhere] * 4,
+        out_specs=[inside] * 4,
         scratch_shapes=[
             pltpu.VMEM(tokens.shape, bf16),
             pltpu.VMEM(out_grad.shape, bf16),
@@ -521,6 +547,7 @@
             pltpu.VMEM((2, 2, half + 1, rows, width // 2), jnp.int16),
             pltpu.VMEM((2, 2, half + 1, 1, width // 2), f32),
             pltpu.VMEM((8, width), f32),
+            pltpu.VMEM((3, 1, margin), f32),
             dma((4,)),
             dma((experts, ONE_CUTS)),
             dma((experts, ONE_CUTS)),
@@ -542,6 +569,8 @@
             dma((2, 2, half)),
             dma,
             dma,
+            dma((3,)),
+            dma((3,)),
         ],
         compiler_params=pltpu.CompilerParams(
             collective_id=0, has_side_effects=True, vmem_limit_bytes=60 * 2**20
@@ -558,21 +587,169 @@
         weight.reshape(1, count),
         routes.reshape(1, count),
         down,
-    )
-
-
-def shifted(block, axis, distance):
-    devices = range(lax.axis_size(axis))
-    route = [(i - distance, i) for i in devices if i - distance in devices]
-    return lax.ppermute(block, axis, route)
-
-
-def cut_window(source, from_index, window_len):
-    return lax.dynamic_slice_in_dim(source, from_index, window_len, 1)
-
-
-def zero_cols(row_count, col_count, kind):
-    return jnp.zeros((row_count, col_count), kind)
+        *states,
+    )
+
+
+def shift_load(ref, offset, row, count):
+    start, lead = offset // 128 + row, lax.rem(offset, 128)
+    lane = lax.broadcasted_iota(jnp.int32, (count, 128), 1)
+    turn = lax.rem(128 - lead, 128)
+    this = pltpu.roll(ref[pl.ds(start, count), :], turn, 1)
+    following = pltpu.roll(ref[pl.ds(start + 1, count), :], turn, 1)
+    return jnp.where(lane < 128 - lead, this, following)
+
+
+def adam(grad, master, moment_one, moment_two):
+    moment_new = beta_one * moment_one + (1.0 - beta_one) * grad
+    square_new = beta_two * moment_two + (1.0 - beta_two) * grad * grad
+    update = (moment_new * (1.0 / (1.0 - beta_one**adam_step))) / (
+        jnp.sqrt(square_new * (1.0 / (1.0 - beta_two**adam_step))) + adam_eps
+    )
+    return master - learn_rate * (update + decay_rate * master), moment_new, square_new
+
+
+def step_kernel(
+    place_ref,
+    block_ref,
+    below_ref,
+    heads_ref,
+    master_ref,
+    one_ref,
+    two_ref,
+    new_master_ref,
+    new_one_ref,
+    new_two_ref,
+    weight_ref,
+    ext,
+    states,
+    made,
+    flat,
+    head_made,
+    block,
+    below,
+    heads,
+    in_sem,
+    out_sem,
+):
+    lead, tail = place_ref[0], place_ref[1]
+    rows, width = block_ref.shape
+    lines = width // 128
+    even = rows * lines
+    slots = master_ref.shape[2] // 128
+    extra = slots - even
+    ahead = 8 * lines
+    sources = (master_ref, one_ref, two_ref)
+    results = (new_master_ref, new_one_ref, new_two_ref)
+    pairs = [(block_ref, block), (below_ref, below)]
+    for i in range(3):
+        pairs.append((sources[i].reshape(slots, 128), states.at[i]))
+        pairs.append((heads_ref.at[i].reshape(heads.shape[1], 128), heads.at[i]))
+    loads = [pltpu.make_async_copy(*pair, in_sem.at[i]) for i, pair in enumerate(pairs)]
+    for load in loads:
+        load.start()
+    for load in loads[:2]:
+        load.wait()
+    for g in range(lines):
+        at = pl.ds(g * 128, 128)
+        ext[pl.ds(g, 8, lines), :] = below[:, at]
+        ext[pl.ds(ahead + g, rows, lines), :] = block[:, at]
+    after = ahead + even
+    ext[pl.ds(after, ext.shape[0] - after), :] = jnp.zeros((ext.shape[0] - after, 128), jnp.float32)
+    held = even * 128 + tail - lead
+    for load in loads[2:]:
+        load.wait()
+
+    def run(row, count):
+        index = (
+            (row + lax.broadcasted_iota(jnp.int32, (count, 128), 0)) * 128
+            + lax.broadcasted_iota(jnp.int32, (count, 128), 1)
+        )
+        inside = index < held
+        grad = jnp.where(inside, shift_load(ext, ahead * 128 + lead, row, count), 0.0)
+        at = pl.ds(row, count)
+        fresh = adam(grad, states[0, at, :], states[1, at, :], states[2, at, :])
+        for i in range(3):
+            made[i, at, :] = jnp.where(inside, fresh[i], 0.0)
+
+    def out(i, first, count):
+        at = pl.ds(first, count)
+        target = results[i].reshape(slots, 128).at[at]
+        return pltpu.make_async_copy(made.at[i, at], target, out_sem.at[i, first // PART])
+
+    parts = [(first, min(PART, slots - first)) for first in range(0, slots, PART)]
+    for first, count in parts:
+        whole = count // 32
+
+        def some(k, _):
+            run(pl.multiple_of(first + k * 32, 8), 32)
+            return 0
+
+        lax.fori_loop(0, whole, some, 0)
+        if count % 32:
+            run(first + whole * 32, count % 32)
+        for i in range(3):
+            out(i, first, count).start()
+
+    head_rows = heads.shape[1]
+    grad = shift_load(ext, (ahead + even) * 128 + tail, 0, head_rows)
+    head_made[pl.ds(0, 32), :] = jnp.zeros((32, 128), jnp.float32)
+    head_made[pl.ds(32, head_rows), :] = adam(grad, heads[0], heads[1], heads[2])[0]
+
+    def lay(row, count):
+        return shift_load(made.at[0], -lead, row, count)
+
+    def some_rows(k, _):
+        row = pl.multiple_of(k * 32, 8)
+        flat[pl.ds(row, 32), :] = lay(row, 32)
+        return 0
+
+    lax.fori_loop(0, even // 32 - 1, some_rows, 0)
+    index = lax.broadcasted_iota(jnp.int32, (32, 128), 0) * 128 + lax.broadcasted_iota(
+        jnp.int32, (32, 128), 1
+    )
+    flat[pl.ds(even - 32, 32), :] = jnp.where(
+        index < 32 * 128 + tail, lay(even - 32, 32), shift_load(head_made, -tail, 0, 32)
+    )
+    for g in range(lines):
+        weight_ref[:, pl.ds(g * 128, 128)] = flat[pl.ds(g, rows, lines), :].astype(jnp.bfloat16)
+    for first, count in parts:
+        for i in range(3):
+            out(i, first, count).wait()
+
+
+PART = 256
+
+
+def bucket_step(places, row_block, below, heads, master, moment_one, moment_two):
+    rows, width = row_block.shape
+    slots = master.shape[2] // 128
+    f32 = jnp.float32
+    inside = pl.BlockSpec(memory_space=pltpu.VMEM)
+    anywhere = pl.BlockSpec(memory_space=pl.ANY)
+    lines = width // 128
+    total = -(-(9 + 8 * lines + slots + 32) // 8) * 8
+    made_rows = -(-(slots + 10) // 8) * 8
+    return pl.pallas_call(
+        step_kernel,
+        out_shape=[jax.ShapeDtypeStruct(master.shape, f32)] * 3
+        + [jax.ShapeDtypeStruct((rows, width), jnp.bfloat16)],
+        in_specs=[pl.BlockSpec(memory_space=pltpu.SMEM)] + [anywhere] * 6,
+        out_specs=[anywhere] * 3 + [inside],
+        scratch_shapes=[
+            pltpu.VMEM((total, 128), f32),
+            pltpu.VMEM((3, slots, 128), f32),
+            pltpu.VMEM((3, made_rows, 128), f32),
+            pltpu.VMEM((rows * lines, 128), f32),
+            pltpu.VMEM((72, 128), f32),
+            pltpu.VMEM(row_block.shape, f32),
+            pltpu.VMEM(below.shape, f32),
+            pltpu.VMEM((3, heads.shape[2] // 128, 128), f32),
+            pltpu.SemaphoreType.DMA((8,)),
+            pltpu.SemaphoreType.DMA((3, -(-slots // PART))),
+        ],
+        compiler_params=pltpu.CompilerParams(vmem_limit_bytes=60 * 2**20),
+    )(places, row_block, below, heads, master, moment_one, moment_two)
 
 
 def shards(
@@ -598,64 +775,32 @@
     n = dp_count // 2
     row_count = token_count * choice_count
     capacity = 2 * row_count // experts
-    row_block, below_rows, router_row = weight_gradient(
+    flat_size = model_width * 2 * hidden
+    even_size = flat_size // dp_count
+    margin_size = bucket_cap - even_size
+    states = (master, moment_one, moment_two)
+    row_block, below_rows, router_row, heads = weight_gradient(
         tokens,
         out_grad,
         gate_up.reshape(row_count, 2 * hidden),
         route_weight,
         routes,
         down_weight[0],
+        states,
+        margin_size,
         n,
         experts,
         capacity,
     )
-    router_grad = router_row.reshape(token_count, choice_count)
-    flat_size = model_width * 2 * hidden
-    even_size = flat_size // dp_count
-    margin_size = bucket_cap - even_size
     position = lax.axis_index("dp")
-    start_at = offsets[position]
-    finish = offsets[position + 1]
-    bucket_len = finish - start_at
-    lead_shift = start_at - position * even_size
-    tail_shift = finish - (position + 1) * even_size
-    slot_ids = jnp.arange(bucket_cap, dtype=jnp.int32)
-    in_bucket = slot_ids < bucket_len
-    row_sum = row_block.reshape(1, even_size)
-    from_below = below_rows.reshape(1, -1)[:, -margin_size:]
-    extended = jnp.concatenate(
-        [from_below, row_sum, zero_cols(local_experts, margin_size, jnp.float32)], axis=1
-    )
-    bucket_grad = cut_window(extended, lead_shift + margin_size, bucket_cap)
-    bucket_grad = jnp.where(in_bucket[None, :], bucket_grad, 0.0)
-    old_master = master[:, 0, :]
-    moment_new = beta_one * moment_one[:, 0, :] + (1.0 - beta_one) * bucket_grad
-    square_new = beta_two * moment_two[:, 0, :] + (1.0 - beta_two) * bucket_grad * bucket_grad
-    update = (
-        moment_new
-        / (1.0 - beta_one**adam_step)
-        / (jnp.sqrt(square_new / (1.0 - beta_two**adam_step)) + adam_eps)
-    )
-    master_new = old_master - learn_rate * (update + decay_rate * old_master)
-    new_master = jnp.where(in_bucket[None, :], master_new, 0.0)
-    new_moment_one = jnp.where(in_bucket[None, :], moment_new, 0.0)
-    new_moment_two = jnp.where(in_bucket[None, :], square_new, 0.0)
-    weight_half = new_master.astype(jnp.bfloat16)
-    head_part = weight_half[:, :margin_size]
-    from_above = shifted(head_part, "dp", -1)
-    from_own = cut_window(weight_half, -lead_shift, even_size)
-    from_next = cut_window(
-        jnp.concatenate([zero_cols(local_experts, even_size, jnp.bfloat16), from_above], axis=1),
-        -tail_shift,
-        even_size,
-    )
-    new_weight = (from_own + from_next).reshape(local_experts, model_width // dp_count, 2 * hidden)
+    places = lax.dynamic_slice(offsets, (position,), (2,)) - even_size * (
+        position + jnp.arange(2, dtype=jnp.int32)
+    )
+    fresh = bucket_step(places, row_block, below_rows, heads, *states)
     return (
-        new_master[:, None, :],
-        new_moment_one[:, None, :],
-        new_moment_two[:, None, :],
-        new_weight,
-        router_grad,
+        *fresh[:3],
+        fresh[3].reshape(1, model_width // dp_count, 2 * hidden),
+        router_row.reshape(token_count, choice_count),
     )
 
 

time: 134 us -> 121 us (0.903)
  other arithmetic: 11.1 us -> 0.58 us
  Pallas kernels: 109 us -> 118 us
  local copies, waits for them, and re-layouts: 6.3 us -> 1.76 us
  starting transfers between devices: 3.97 us -> 0 us
  between operations: 3.38 us -> 0.67 us
    pallas_call x0 -> x1, Pallas kernels: none -> 8.62 us  [bucket_step(): pl.pallas_call(step_kernel, out_shape=[jax.ShapeDtypeStruct(master.shape,...]
    convert_element_type x1 -> x0, other arithmetic: 5.99 us -> none  [shards(): weight_half = new_master.astype(jnp.bfloat16)]
    ppermute x1 -> x0, starting transfers between devices: 3.97 us -> none  [shifted(): return lax.ppermute(block, axis, route)]
    broadcast_in_dim x1 -> x0, other arithmetic: 2.78 us -> none  [shards(): new_moment_two[:, None, :]]
    unnamed x13 -> x5, local copies, waits for them, and re-layouts: 4.3 us -> 1.76 us
    add x1 -> x0, other arithmetic: 2.34 us -> none  [shards(): from_own + from_next]
  transfers between devices with their start and end apart: 1 -> 0, of which waited for: 0 -> 0; matrix products, arithmetic and copies ran while one was open for 2% -> 0% of each run, Pallas kernels for 0% -> 0%
where the time goes in v4:
time: 121 us
  Pallas kernels  118 us (98%)
  local copies, waits for them, and re-layouts  1.76 us (1%)
    pallas_call x1, Pallas kernels, weight_gradient(): pl.pallas_call(functools.partial(grad_kernel, n, experts), out_shape=(jax...  109 us
    pallas_call x1, Pallas kernels, bucket_step(): pl.pallas_call(step_kernel, out_shape=[jax.ShapeDtypeStruct(master.shape,...  8.62 us

profile of v4, /device:TPU:1, one launch (start us, length us, event | category | flops | bytes accessed | tf_op | source)
XLA Modules:
  0.0 120.5 jit_solution(16610957575585372083)
XLA Ops:
  0.6 0.0 copy-start
  0.6 0.6 copy-done
  1.3 0.6 multiply_subtract_fusion.place_ref
  1.9 108.9 %shard_map.137 = (f32[80,1536]{1,0:T(8,128)}, f32[8,1536]{1,0:T(8,128)}, f32[1,128]{1,0:T(1,128)}, f32[3,1,3840]{2,1,0:T(1,128)}) custom-call(bf16[128,2560]{1,0:T(8,128)(2,1)} %tok_ref.1, bf16[128,2560]{1,0:T(8,128)(2,1)} %grad_ref.1, bf16[128,1536]{1,0:T(8,128)(2,1)} %bitcast.6, bf16[1,128]{1,0:T(2,128)(2,1)} %bitcast.9, s32[1,128]{1,0:T(1,128)} %bitcast.10, ...), custom_call_target="tpu_custom_call" | custom-call | flops 3296722944 | bytes 1081344 | tf_op jit(solution)/shard_map/pallas_call | solution.py:518
  110.8 8.6 %shard_map.138 = (f32[1,1,126720]{2,1,0:T(1,128)}, f32[1,1,126720]{2,1,0:T(1,128)}, f32[1,1,126720]{2,1,0:T(1,128)}, bf16[80,1536]{1,0:T(8,128)(2,1)}) custom-call(s32[2]{0:T(128)} %multiply_subtract_fusion.place_ref, f32[80,1536]{1,0:T(8,128)} %get-tuple-element.13.block_ref, f32[8,1536]{1,0:T(8,128)} %get-tuple-element.14.below_ref, ...), custom_call_target="tpu_custom_call" | custom-call | tf_op jit(solution)/shard_map/pallas_call | solution.py:733
  119.4 0.0 copy-start.1
  119.4 0.6 copy-done.1
  120.0 0.5 copy.16
Async XLA Ops:
  0.6 0.7 copy-start
  119.4 0.6 copy-start.1

commit v5 on v4

--- a/solution.py
+++ b/solution.py
@@ -18,12 +18,21 @@
 
 
 ONE_CUTS = 3
-TWO_CUTS = 2
+TWO_CUTS = 4
 
 
 def distance(i, side):
     dx, dy = i // side, i % side
     return min(dx, 4 - dx) + min(dy, side - dy), -min(dx, 4 - dx), -min(i, 16 - i)
+
+
+def groups_needed(t, span):
+    most = 0
+    for w in range(span):
+        delta = 3 - 2 * ((2 * w) // span)
+        order = [0, delta, 4 - delta, 2]
+        most = max(most, *(order.index((w + way * t) // span % 4) for way in (-1, 1)))
+    return most + 1
 
 
 def grad_kernel(
@@ -73,6 +82,8 @@
     ring_recv,
     pass_send,
     pass_recv,
+    twin_send,
+    twin_recv,
     first_send,
     first_recv,
     score_send,
@@ -103,9 +114,20 @@
     other = (z * 2 + 1 - c, me)
     ahead = (lax.rem(z + 1, n) * 2 + c, me)
     behind = (lax.rem(z + n - 1, n) * 2 + c, me)
+    ahead_twin = (lax.rem(z + 1, n) * 2 + 1 - c, me)
+    behind_twin = (lax.rem(z + n - 1, n) * 2 + 1 - c, me)
     upper = (lax.rem(dp + 1, 2 * n), me)
     lower = (lax.rem(dp + 2 * n - 1, 2 * n), me)
     every = ((0, 0), (1, 1), (0, 1), (1, 0))
+    span = n // TWO_CUTS
+    group = depth // TWO_CUTS
+    farthest = lax.rem(z + half, n)
+    delta = 3 - 2 * ((2 * lax.rem(farthest, span)) // span)
+    order = [lax.rem(farthest // span + turn, 4) for turn in (0, delta, 4 - delta, 2)]
+
+    def group_at(p):
+        return pl.ds(pl.multiple_of(order[p] * group, 128), group)
+
 
     def peer_at(dx, dy):
         x = lax.rem(me // side + dx + 4 * side, experts // side)
@@ -127,7 +149,7 @@
         )
 
     barrier = pltpu.get_barrier_semaphore()
-    for device in (other, ahead, behind, upper, lower):
+    for device in (other, ahead, behind, ahead_twin, behind_twin):
         pl.semaphore_signal(barrier, inc=1, device_id=device, device_id_type=MESH)
 
     def greet(i, _):
@@ -161,6 +183,12 @@
         return remote(
             block, block, ring_send.at[d, u, s], ring_recv.at[d, u, s], (ahead, behind)[d]
         )
+
+    def twin_copy(d):
+        s = half - 1
+        block = down_all.at[c, place(z - s if d == 0 else z + s), pl.ds(d * part, part)]
+        device = (ahead_twin, behind_twin)[d]
+        return remote(block, block, twin_send.at[d], twin_recv.at[d], device)
 
     def pass_copy(r, half_at):
         block = down_all.at[half_at, place(z + r)]
@@ -208,8 +236,7 @@
         )
 
     def two_copy(i, p):
-        size = pack_two.shape[1] // TWO_CUTS
-        at = pl.ds(pl.multiple_of(p * size, 128), size)
+        at = group_at(p)
         return remote(
             pack_two.at[block(peer(i)), at],
             feats.at[block(me), at],
@@ -235,52 +262,55 @@
     pack_one[:, pl.ds(depth + 2 * hidden, 128)] = jnp.broadcast_to(
         slot_weight, (experts * slots, 128)
     ).astype(jnp.bfloat16)
+    def share_first():
+        first.wait()
+        mine = down_wide[:, pl.ds(pl.multiple_of(c * 2 * part, 128), 2 * part)]
+        theirs = down_sib[...]
+        top, low = jnp.where(c == 0, mine, theirs), jnp.where(c == 0, theirs, mine)
+        down_all[c, place(z), :] = jnp.concatenate([top, low], axis=0).astype(jnp.bfloat16)
+        for d, u in every:
+            down_copy(d, u, 0).start()
+        pass_copy(0, c).start()
+
+    def forward(s):
+        if s >= half:
+            return
+        for d, u in every:
+            down_copy(d, u, s - 1).wait_recv()
+            if d == u or s < half - 1:
+                down_copy(d, u, s).start()
+            if d == u and s == half - 1:
+                twin_copy(d).start()
+        pass_copy(n - s, c).start()
+        pass_copy(s, c).start()
+
     loads[1].wait()
     loads[2].wait()
-    pack(pack_one, ONE_CUTS, 0, (grad_in, saved_in))
-    for i in far:
-        one_copy(i, 0).start()
-    first.wait()
-    mine = down_wide[:, pl.ds(pl.multiple_of(c * 2 * part, 128), 2 * part)]
-    theirs = down_sib[...]
-    top, low = jnp.where(c == 0, mine, theirs), jnp.where(c == 0, theirs, mine)
-    down_all[c, place(z), :] = jnp.concatenate([top, low], axis=0).astype(jnp.bfloat16)
-    for d, u in every:
-        down_copy(d, u, 0).start()
-    pass_copy(0, c).start()
-    for p in range(1, ONE_CUTS):
+    for p in range(ONE_CUTS):
         pack(pack_one, ONE_CUTS, p, (grad_in, saved_in))
+        if p == 0:
+            share_first()
         for i in far:
             one_copy(i, p).start()
+        forward(p + 1)
     loads[3].wait()
     for p in range(TWO_CUTS):
-        pack(pack_two, TWO_CUTS, p, (tok_in,))
+        pack_two[:, group_at(p)] = jnp.dot(
+            select, tok_in[:, group_at(p)], preferred_element_type=jnp.float32
+        ).astype(jnp.bfloat16)
         for i in far:
             two_copy(i, p).start()
+        forward(p + ONE_CUTS + 1)
     for i in range(3):
         head_copy(i).start()
     rows_in[block(me), :] = pack_one[block(me), :]
     feats[block(me), :] = pack_two[block(me), :]
 
-    def forward(s, _):
-        for d, u in every:
-            down_copy(d, u, s - 1).wait_recv()
-            if d == u:
-                down_copy(d, u, s).start()
-            else:
-
-                @pl.when(s < half - 1)
-                def _():
-                    down_copy(d, u, s).start()
-
-        pass_copy(n - s, c).start()
-        pass_copy(s, c).start()
-        return 0
-
-    lax.fori_loop(1, half, forward, 0)
+    for s in range(ONE_CUTS + TWO_CUTS + 1, half):
+        forward(s)
     for u in range(2):
         down_copy(u, u, half - 1).wait_recv()
-    pass_copy(half, c).start()
+        twin_copy(u).wait_recv()
 
     def land_one(i, _):
         for p in range(ONE_CUTS):
@@ -293,7 +323,8 @@
         pass_copy(r, 1 - c).wait_recv()
         return 0
 
-    lax.fori_loop(0, n, land_pass, 0)
+    lax.fori_loop(0, half, land_pass, 0)
+    lax.fori_loop(half + 1, n, land_pass, 0)
 
     tile = 256
     weight = rows_in[:, pl.ds(depth + 2 * hidden, 128)].astype(jnp.float32)[:, :1]
@@ -329,14 +360,14 @@
             (dp, peer(i)),
         )
 
-    def land_two(i, _):
-        for p in range(TWO_CUTS):
+    def land_two(p):
+        def land(i, _):
             two_copy(i, p).wait_recv()
-        return 0
-
-    lax.fori_loop(1, experts, land_two, 0)
-    for i in range(depth // 256):
-        feat_t[pl.ds(i * 256, 256), :] = feats[:, pl.ds(i * 256, 256)].T
+            return 0
+
+        lax.fori_loop(1, experts, land, 0)
+        at = group_at(p)
+        feat_t[at, :] = feats[:, at].T
 
     def sib_copy(r):
         return remote(give.at[r], sib.at[r], sib_send.at[r], sib_recv.at[r], other)
@@ -395,8 +426,13 @@
             for copy in ring_copy(d, u, s):
                 copy.start()
 
+    groups = [groups_needed(t, span) for t in range(half + 1)]
+    for p in range(groups[0]):
+        land_two(p)
     produce([half])
     sib_copy(half).start()
+    for p in range(groups[0], groups[1]):
+        land_two(p)
     produce([half - 1, half + 1])
     sib_copy(half - 1).start()
     sib_copy(half + 1).start()
@@ -424,6 +460,12 @@
         def _():
             step(s, every, ())
 
+        for p in range(groups[1], TWO_CUTS):
+
+            @pl.when(s + 1 == min(t for t in range(half + 1) if groups[t] > p))
+            def _():
+                land_two(p)
+
         @pl.when(k > 1)
         def _():
             produce([k - 1, n - k + 1])
@@ -459,7 +501,8 @@
         pass_copy(r, c).wait_send()
         return 0
 
-    lax.fori_loop(0, n, drain_pass, 0)
+    lax.fori_loop(0, half, drain_pass, 0)
+    lax.fori_loop(half + 1, n, drain_pass, 0)
 
     def drain_down(s, _):
         for d, u in every:
@@ -469,6 +512,7 @@
     lax.fori_loop(0, half - 1, drain_down, 0)
     for u in range(2):
         down_copy(u, u, half - 1).wait_send()
+        twin_copy(u).wait_send()
 
     def drain_sum(s, _):
         for d, u in every:
@@ -557,6 +601,8 @@
             dma((2, 2, half)),
             dma((n,)),
             dma((n,)),
+            dma((2,)),
+            dma((2,)),
             dma,
             dma,
             dma((experts,)),
@@ -610,17 +656,19 @@
 
 
 def step_kernel(
-    place_ref,
+    offset_ref,
     block_ref,
     below_ref,
     heads_ref,
     master_ref,
     one_ref,
     two_ref,
+    router_ref,
     new_master_ref,
     new_one_ref,
     new_two_ref,
     weight_ref,
+    new_router_ref,
     ext,
     states,
     made,
@@ -632,16 +680,18 @@
     in_sem,
     out_sem,
 ):
-    lead, tail = place_ref[0], place_ref[1]
     rows, width = block_ref.shape
     lines = width // 128
     even = rows * lines
+    position = lax.axis_index("dp")
+    lead = offset_ref[position] - position * (even * 128)
+    tail = offset_ref[position + 1] - (position + 1) * (even * 128)
     slots = master_ref.shape[2] // 128
     extra = slots - even
     ahead = 8 * lines
     sources = (master_ref, one_ref, two_ref)
     results = (new_master_ref, new_one_ref, new_two_ref)
-    pairs = [(block_ref, block), (below_ref, below)]
+    pairs = [(block_ref, block), (below_ref, below), (router_ref, new_router_ref)]
     for i in range(3):
         pairs.append((sources[i].reshape(slots, 128), states.at[i]))
         pairs.append((heads_ref.at[i].reshape(heads.shape[1], 128), heads.at[i]))
@@ -685,7 +735,7 @@
             run(pl.multiple_of(first + k * 32, 8), 32)
             return 0
 
-        lax.fori_loop(0, whole, some, 0)
+        lax.fori_loop(0, whole, some, 0, unroll=True)
         if count % 32:
             run(first + whole * 32, count % 32)
         for i in range(3):
@@ -704,7 +754,7 @@
         flat[pl.ds(row, 32), :] = lay(row, 32)
         return 0
 
-    lax.fori_loop(0, even // 32 - 1, some_rows, 0)
+    lax.fori_loop(0, even // 32 - 1, some_rows, 0, unroll=True)
     index = lax.broadcasted_iota(jnp.int32, (32, 128), 0) * 128 + lax.broadcasted_iota(
         jnp.int32, (32, 128), 1
     )
@@ -721,7 +771,7 @@
 PART = 256
 
 
-def bucket_step(places, row_block, below, heads, master, moment_one, moment_two):
+def bucket_step(offsets, row_block, below, heads, master, moment_one, moment_two, router):
     rows, width = row_block.shape
     slots = master.shape[2] // 128
     f32 = jnp.float32
@@ -733,9 +783,12 @@
     return pl.pallas_call(
         step_kernel,
         out_shape=[jax.ShapeDtypeStruct(master.shape, f32)] * 3
-        + [jax.ShapeDtypeStruct((rows, width), jnp.bfloat16)],
-        in_specs=[pl.BlockSpec(memory_space=pltpu.SMEM)] + [anywhere] * 6,
-        out_specs=[anywhere] * 3 + [inside],
+        + [
+            jax.ShapeDtypeStruct((rows, width), jnp.bfloat16),
+            jax.ShapeDtypeStruct(router.shape, f32),
+        ],
+        in_specs=[pl.BlockSpec(memory_space=pltpu.SMEM)] + [anywhere] * 7,
+        out_specs=[anywhere] * 3 + [inside, anywhere],
         scratch_shapes=[
             pltpu.VMEM((total, 128), f32),
             pltpu.VMEM((3, slots, 128), f32),
@@ -745,11 +798,11 @@
             pltpu.VMEM(row_block.shape, f32),
             pltpu.VMEM(below.shape, f32),
             pltpu.VMEM((3, heads.shape[2] // 128, 128), f32),
-            pltpu.SemaphoreType.DMA((8,)),
+            pltpu.SemaphoreType.DMA((9,)),
             pltpu.SemaphoreType.DMA((3, -(-slots // PART))),
         ],
         compiler_params=pltpu.CompilerParams(vmem_limit_bytes=60 * 2**20),
-    )(places, row_block, below, heads, master, moment_one, moment_two)
+    )(offsets, row_block, below, heads, master, moment_one, moment_two, router)
 
 
 def shards(
@@ -792,15 +845,11 @@
         experts,
         capacity,
     )
-    position = lax.axis_index("dp")
-    places = lax.dynamic_slice(offsets, (position,), (2,)) - even_size * (
-        position + jnp.arange(2, dtype=jnp.int32)
-    )
-    fresh = bucket_step(places, row_block, below_rows, heads, *states)
+    fresh = bucket_step(offsets, row_block, below_rows, heads, *states, router_row)
     return (
         *fresh[:3],
         fresh[3].reshape(1, model_width // dp_count, 2 * hidden),
-        router_row.reshape(token_count, choice_count),
+        fresh[4].reshape(token_count, choice_count),
     )
 
 

time: 121 us -> 110 us (0.909)
  Pallas kernels: 118 us -> 109 us
  local copies, waits for them, and re-layouts: 1.76 us -> 0 us
    pallas_call x1, Pallas kernels: 109 us -> 105 us  [weight_gradient(): pl.pallas_call(functools.partial(grad_kernel, n, experts), out_shape=(jax...]
    pallas_call x1, Pallas kernels: 8.62 us -> 4.68 us  [bucket_step(): pl.pallas_call(step_kernel, out_shape=[jax.ShapeDtypeStruct(master.shape,...]
    unnamed x5 -> x0, local copies, waits for them, and re-layouts: 1.76 us -> none
where the time goes in v5:
time: 110 us
  Pallas kernels  109 us (99%)
    pallas_call x1, Pallas kernels, weight_gradient(): pl.pallas_call(functools.partial(grad_kernel, n, experts), out_shape=(jax...  105 us
    pallas_call x1, Pallas kernels, bucket_step(): pl.pallas_call(step_kernel, out_shape=[jax.ShapeDtypeStruct(master.shape,...  4.68 us

profile of v5, /device:TPU:1, one launch (start us, length us, event | category | flops | bytes accessed | tf_op | source)
XLA Modules:
  0.0 109.9 jit_solution(4774077737178565132)
XLA Ops:
  0.6 104.6 %shard_map.137 = (f32[80,1536]{1,0:T(8,128)}, f32[8,1536]{1,0:T(8,128)}, f32[1,128]{1,0:T(1,128)}, f32[3,1,3840]{2,1,0:T(1,128)}) custom-call(bf16[128,2560]{1,0:T(8,128)(2,1)} %tok_ref.1, bf16[128,2560]{1,0:T(8,128)(2,1)} %grad_ref.1, bf16[128,1536]{1,0:T(8,128)(2,1)} %bitcast.6, bf16[1,128]{1,0:T(2,128)(2,1)} %bitcast.9, s32[1,128]{1,0:T(1,128)} %bitcast.10, ...), custom_call_target="tpu_custom_call" | custom-call | flops 3296722944 | bytes 1081344 | tf_op jit(solution)/shard_map/pallas_call | solution.py:562
  105.2 4.7 %shard_map.138 = (f32[1,1,126720]{2,1,0:T(1,128)}, f32[1,1,126720]{2,1,0:T(1,128)}, f32[1,1,126720]{2,1,0:T(1,128)}, bf16[80,1536]{1,0:T(8,128)(2,1)}, f32[1,128]{1,0:T(1,128)}) custom-call(s32[33]{0:T(128)} %offset_ref.1, f32[80,1536]{1,0:T(8,128)} %get-tuple-element.14.block_ref, f32[8,1536]{1,0:T(8,128)} %get-tuple-element.15.below_ref, ...), custom_call_target="tpu_custom_call" | custom-call | tf_op jit(solution)/shard_map/pallas_call | solution.py:783

commit v6 on v5

--- a/solution.py
+++ b/solution.py
@@ -59,8 +59,9 @@
     pack_two,
     rows_in,
     feats,
-    down_wide,
-    down_sib,
+    raw,
+    raw_in,
+    raw_sib,
     down_all,
     dgu,
     score,
@@ -86,6 +87,8 @@
     twin_recv,
     first_send,
     first_recv,
+    raw_send,
+    raw_recv,
     score_send,
     score_recv,
     sib_send,
@@ -94,6 +97,8 @@
     sum_recv,
     scale_send,
     scale_recv,
+    rest_send,
+    rest_recv,
     tail_send,
     tail_recv,
     head_send,
@@ -167,13 +172,29 @@
     for load in loads:
         load.start()
 
-    first = remote(
-        down_wide.at[:, pl.ds(pl.multiple_of((1 - c) * 2 * part, 128), 2 * part)],
-        down_sib,
-        first_send,
-        first_recv,
-        other,
-    )
+    def half_at(h):
+        return pl.ds(pl.multiple_of(h * 2 * part, 128), 2 * part)
+
+    first = remote(raw.at[:, half_at(1 - c)], raw_sib, first_send, first_recv, other)
+
+    def raw_copy(d, h):
+        chip = lax.rem(z + (1, n - 1)[d], n)
+        return remote(
+            raw.at[:, half_at(h)],
+            raw_in.at[d, c],
+            raw_send.at[d, h],
+            raw_recv.at[d, c],
+            (chip * 2 + h, me),
+        )
+
+    def raw_land(d, core):
+        return remote(
+            raw.at[:, half_at(core)],
+            raw_in.at[d, core],
+            raw_send.at[d, core],
+            raw_recv.at[d, core],
+            (ahead, behind)[d],
+        )
 
     def place(idx):
         return pl.ds(pl.multiple_of(lax.rem(idx + n, n) * 2 * share, 16), 2 * share)
@@ -256,27 +277,44 @@
         )
 
     loads[0].wait()
-    down_wide[...] = down_in[...].astype(jnp.float32)
+    shard = down_in[...].astype(jnp.float32)
+    if raw.shape[0] > share:
+        spare = jnp.zeros((raw.shape[0] - share, depth), jnp.float32)
+        shard = jnp.concatenate([shard, spare], axis=0)
+    raw[...] = shard.astype(jnp.bfloat16)
     pl.semaphore_wait(barrier, experts + 4)
+    for h in range(2):
+        for d in range(2):
+            raw_copy(d, h).start()
     first.start()
     pack_one[:, pl.ds(depth + 2 * hidden, 128)] = jnp.broadcast_to(
         slot_weight, (experts * slots, 128)
     ).astype(jnp.bfloat16)
+    def joined(top, low):
+        pieces = [top.astype(jnp.float32)[:share], low.astype(jnp.float32)[:share]]
+        return jnp.concatenate(pieces, axis=0).astype(jnp.bfloat16)
+
     def share_first():
         first.wait()
-        mine = down_wide[:, pl.ds(pl.multiple_of(c * 2 * part, 128), 2 * part)]
-        theirs = down_sib[...]
-        top, low = jnp.where(c == 0, mine, theirs), jnp.where(c == 0, theirs, mine)
-        down_all[c, place(z), :] = jnp.concatenate([top, low], axis=0).astype(jnp.bfloat16)
-        for d, u in every:
-            down_copy(d, u, 0).start()
+        mine = raw[:, half_at(c)].astype(jnp.float32)
+        theirs = raw_sib[...].astype(jnp.float32)
+        down_all[c, place(z), :] = joined(
+            jnp.where(c == 0, mine, theirs), jnp.where(c == 0, theirs, mine)
+        )
         pass_copy(0, c).start()
 
     def forward(s):
         if s >= half:
             return
+        if s == 1:
+            for d in range(2):
+                raw_land(d, 0).wait_recv()
+                raw_land(d, 1).wait_recv()
+                block_at = place(z - 1 if d == 0 else z + 1)
+                down_all[c, block_at, :] = joined(raw_in[d, 0], raw_in[d, 1])
         for d, u in every:
-            down_copy(d, u, s - 1).wait_recv()
+            if s > 1:
+                down_copy(d, u, s - 1).wait_recv()
             if d == u or s < half - 1:
                 down_copy(d, u, s).start()
             if d == u and s == half - 1:
@@ -387,6 +425,24 @@
             )
         ]
 
+    late, early = pl.ds(rows - 16, 16), pl.ds(0, rows - 16)
+
+    def last_copy(d, u, pieces=(0, 1, 2)):
+        s = half - 1
+        parts = (
+            (scale.at[d, u, s], scale.at[d, u, s + 1], scale_send, scale_recv),
+            (work.at[d, u, s, late], work.at[d, u, s + 1, late], sum_send, sum_recv),
+            (work.at[d, u, s, early], work.at[d, u, s + 1, early], rest_send, rest_recv),
+        )
+        copies = []
+        for i in pieces:
+            source, target, send, recv = parts[i]
+            slot = (d, u) if i == 2 else (d, u, s)
+            copies.append(
+                remote(source, target, send.at[slot], recv.at[slot], (ahead, behind)[d])
+            )
+        return copies
+
     def produce(places):
         pieces = []
         for r in places:
@@ -403,14 +459,14 @@
                 own[r, :, at] = prod[2 * i * rows : (2 * i + 1) * rows]
                 give[r, :, at] = prod[(2 * i + 1) * rows : (2 * i + 2) * rows]
 
-    def chip_sum(r, u):
-        at = pl.ds(u * cols, cols)
-        return own[r, :, at].astype(jnp.float32) + sib[r, :, at].astype(jnp.float32)
-
-    def decoded(d, u, s):
-        return work[d, u, s].astype(jnp.int32).astype(jnp.float32) * scale[d, u, s]
-
-    def step(s, streams, fresh):
+    def chip_sum(r, u, at=pl.ds(0, rows)):
+        across = pl.ds(u * cols, cols)
+        return own[r, at, across].astype(jnp.float32) + sib[r, at, across].astype(jnp.float32)
+
+    def decoded(d, u, s, at=pl.ds(0, rows)):
+        return work[d, u, s, at, :].astype(jnp.int32).astype(jnp.float32) * scale[d, u, s]
+
+    def step(s, streams, fresh, last=False):
         k = half - s
         for d, u in streams:
             r = k if d == 0 else n - k
@@ -423,21 +479,27 @@
             scale[d, u, s] = most * (1.0 / 32767.0)
             coded = jnp.round(value * (32767.0 / most))
             work[d, u, s] = coded.astype(jnp.int32).astype(jnp.int16)
-            for copy in ring_copy(d, u, s):
+            for copy in last_copy(d, u) if last else ring_copy(d, u, s):
                 copy.start()
 
     groups = [groups_needed(t, span) for t in range(half + 1)]
-    for p in range(groups[0]):
-        land_two(p)
-    produce([half])
-    sib_copy(half).start()
-    for p in range(groups[0], groups[1]):
-        land_two(p)
-    produce([half - 1, half + 1])
-    sib_copy(half - 1).start()
-    sib_copy(half + 1).start()
+    needed = [min(t for t in range(half + 1) if groups[t] > p) for p in range(TWO_CUTS)]
+
+    def prepare(t):
+        for p in range(TWO_CUTS):
+            if needed[p] == t:
+                land_two(p)
+        k = half - t
+        places = [k] if k in (0, half) else [k, n - k]
+        produce(places)
+        for r in places:
+            sib_copy(r).start()
+
+    prepare(0)
+    prepare(1)
     sib_copy(half).wait_recv()
     step(0, every[:2], every[:2])
+    prepare(2)
 
     def send_score(i, _):
         score_copy(i).start()
@@ -460,23 +522,26 @@
         def _():
             step(s, every, ())
 
-        for p in range(groups[1], TWO_CUTS):
-
-            @pl.when(s + 1 == min(t for t in range(half + 1) if groups[t] > p))
-            def _():
-                land_two(p)
-
-        @pl.when(k > 1)
-        def _():
-            produce([k - 1, n - k + 1])
-            sib_copy(k - 1).start()
-            sib_copy(n - k + 1).start()
-
-        return 0
-
-    lax.fori_loop(1, half, body, 0)
-    produce([0])
-    sib_copy(0).start()
+        for p in range(TWO_CUTS):
+            if needed[p] > 2:
+
+                @pl.when(s + 2 == needed[p])
+                def _():
+                    land_two(p)
+
+        produce([k - 2, n - k + 2])
+        sib_copy(k - 2).start()
+        sib_copy(n - k + 2).start()
+        return 0
+
+    lax.fori_loop(1, half - 2, body, 0)
+    for s in range(max(1, half - 2), half):
+        k = half - s
+        sib_copy(k).wait_recv()
+        sib_copy(n - k).wait_recv()
+        step(s, every, every[2:] if s == 1 else (), s == half - 1)
+        if k == 2:
+            prepare(half)
 
     def land_score(i, _):
         score_copy(i).wait()
@@ -509,7 +574,10 @@
             down_copy(d, u, s).wait_send()
         return 0
 
-    lax.fori_loop(0, half - 1, drain_down, 0)
+    lax.fori_loop(1, half - 1, drain_down, 0)
+    for d in range(2):
+        for h in range(2):
+            raw_copy(d, h).wait_send()
     for u in range(2):
         down_copy(u, u, half - 1).wait_send()
         twin_copy(u).wait_send()
@@ -525,22 +593,29 @@
             copy.wait_send()
     lax.fori_loop(1, half - 1, drain_sum, 0)
     sib_copy(0).wait_recv()
-    for u in range(2):
-        for d in range(2):
-            for copy in ring_copy(d, u, half - 1):
-                copy.wait_recv()
-        out_ref[:, pl.ds(u * cols, cols)] = chip_sum(0, u) + (
-            decoded(0, u, half) + decoded(1, u, half)
-        )
+
+    def finish(at, pieces):
+        for u in range(2):
+            for d in range(2):
+                for copy in last_copy(d, u, pieces):
+                    copy.wait_recv()
+            out_ref[at, pl.ds(u * cols, cols)] = chip_sum(0, u, at) + (
+                decoded(0, u, half, at) + decoded(1, u, half, at)
+            )
+
+    finish(late, (0, 1))
     last = remote(out_ref.at[pl.ds(rows - 8, 8)], tail_in, tail_send, tail_recv, upper)
     last.start()
+    finish(early, (2,))
 
     def drain_sib(r, _):
         sib_copy(r).wait_send()
         return 0
 
     lax.fori_loop(0, n, drain_sib, 0)
-    drain_sum(half - 1, 0)
+    for d, u in every:
+        for copy in last_copy(d, u):
+            copy.wait_send()
     last.wait()
     tail_ref[...] = tail_in[...]
 
@@ -555,6 +630,7 @@
     rows = depth // (2 * n)
     half = n // 2
     wide = depth + width + 128
+    padded = -(-down.shape[0] // 16) * 16
     dma = pltpu.SemaphoreType.DMA
     bf16, f32 = jnp.bfloat16, jnp.float32
     anywhere = pl.BlockSpec(memory_space=pl.ANY)
@@ -578,8 +654,9 @@
             pltpu.VMEM((total, depth), bf16),
             pltpu.VMEM((total, wide), bf16),
             pltpu.VMEM((total, depth), bf16),
-            pltpu.VMEM(down.shape, f32),
-            pltpu.VMEM((down.shape[0], depth // 2), f32),
+            pltpu.VMEM((padded, depth), bf16),
+            pltpu.VMEM((2, 2, padded, depth // 2), bf16),
+            pltpu.VMEM((padded, depth // 2), bf16),
             pltpu.VMEM((2, hidden, depth // 2), bf16),
             pltpu.VMEM((total, width), bf16),
             pltpu.VMEM((total, count), f32),
@@ -605,6 +682,8 @@
             dma((2,)),
             dma,
             dma,
+            dma((2, 2)),
+            dma((2, 2)),
             dma((experts,)),
             dma((experts,)),
             dma((n,)),
@@ -613,6 +692,8 @@
             dma((2, 2, half)),
             dma((2, 2, half)),
             dma((2, 2, half)),
+            dma((2, 2)),
+            dma((2, 2)),
             dma,
             dma,
             dma((3,)),

time: 110 us -> 108 us (0.982)
  Pallas kernels: 109 us -> 107 us
    pallas_call x1, Pallas kernels: 105 us -> 103 us  [weight_gradient(): pl.pallas_call(functools.partial(grad_kernel, n, experts), out_shape=(jax...]
where the time goes in v6:
time: 108 us
  Pallas kernels  107 us (99%)
    pallas_call x1, Pallas kernels, weight_gradient(): pl.pallas_call(functools.partial(grad_kernel, n, experts), out_shape=(jax...  103 us
    pallas_call x1, Pallas kernels, bucket_step(): pl.pallas_call(step_kernel, out_shape=[jax.ShapeDtypeStruct(master.shape,...  4.68 us

profile of v6, /device:TPU:1, one launch (start us, length us, event | category | flops | bytes accessed | tf_op | source)
XLA Modules:
  0.0 107.9 jit_solution(11706434903302597181)
XLA Ops:
  0.6 102.5 %shard_map.137 = (f32[80,1536]{1,0:T(8,128)}, f32[8,1536]{1,0:T(8,128)}, f32[1,128]{1,0:T(1,128)}, f32[3,1,3840]{2,1,0:T(1,128)}) custom-call(bf16[128,2560]{1,0:T(8,128)(2,1)} %tok_ref.1, bf16[128,2560]{1,0:T(8,128)(2,1)} %grad_ref.1, bf16[128,1536]{1,0:T(8,128)(2,1)} %bitcast.6, bf16[1,128]{1,0:T(2,128)(2,1)} %bitcast.9, s32[1,128]{1,0:T(1,128)} %bitcast.10, ...), custom_call_target="tpu_custom_call" | custom-call | flops 3296722944 | bytes 1081344 | tf_op jit(solution)/shard_map/pallas_call | solution.py:638
  103.2 4.7 %shard_map.138 = (f32[1,1,126720]{2,1,0:T(1,128)}, f32[1,1,126720]{2,1,0:T(1,128)}, f32[1,1,126720]{2,1,0:T(1,128)}, bf16[80,1536]{1,0:T(8,128)(2,1)}, f32[1,128]{1,0:T(1,128)}) custom-call(s32[33]{0:T(128)} %offset_ref.1, f32[80,1536]{1,0:T(8,128)} %get-tuple-element.14.block_ref, f32[8,1536]{1,0:T(8,128)} %get-tuple-element.15.below_ref, ...), custom_call_target="tpu_custom_call" | custom-call | tf_op jit(solution)/shard_map/pallas_call | solution.py:864

commit v7 on v6

--- a/solution.py
+++ b/solution.py
@@ -153,16 +153,6 @@
             device_id_type=MESH,
         )
 
-    barrier = pltpu.get_barrier_semaphore()
-    for device in (other, ahead, behind, ahead_twin, behind_twin):
-        pl.semaphore_signal(barrier, inc=1, device_id=device, device_id_type=MESH)
-
-    def greet(i, _):
-        pl.semaphore_signal(barrier, inc=1, device_id=(dp, peer(i)), device_id_type=MESH)
-        return 0
-
-    lax.fori_loop(1, experts, greet, 0)
-
     loads = [
         pltpu.make_async_copy(source, target, load_sem.at[i])
         for i, (source, target) in enumerate(
@@ -171,6 +161,16 @@
     ]
     for load in loads:
         load.start()
+
+    barrier = pltpu.get_barrier_semaphore()
+    for device in (other, ahead, behind, ahead_twin, behind_twin):
+        pl.semaphore_signal(barrier, inc=1, device_id=device, device_id_type=MESH)
+
+    def greet(i, _):
+        pl.semaphore_signal(barrier, inc=1, device_id=(dp, peer(i)), device_id_type=MESH)
+        return 0
+
+    lax.fori_loop(1, experts, greet, 0)
 
     def half_at(h):
         return pl.ds(pl.multiple_of(h * 2 * part, 128), 2 * part)
@@ -346,9 +346,6 @@
 
     for s in range(ONE_CUTS + TWO_CUTS + 1, half):
         forward(s)
-    for u in range(2):
-        down_copy(u, u, half - 1).wait_recv()
-        twin_copy(u).wait_recv()
 
     def land_one(i, _):
         for p in range(ONE_CUTS):
@@ -361,8 +358,13 @@
         pass_copy(r, 1 - c).wait_recv()
         return 0
 
-    lax.fori_loop(0, half, land_pass, 0)
-    lax.fori_loop(half + 1, n, land_pass, 0)
+    lax.fori_loop(0, half - 1, land_pass, 0)
+    lax.fori_loop(half + 2, n, land_pass, 0)
+    for u in range(2):
+        down_copy(u, u, half - 1).wait_recv()
+        twin_copy(u).wait_recv()
+    land_pass(half - 1, 0)
+    land_pass(half + 1, 0)
 
     tile = 256
     weight = rows_in[:, pl.ds(depth + 2 * hidden, 128)].astype(jnp.float32)[:, :1]
@@ -509,6 +511,60 @@
     mine_at = pl.ds(pl.multiple_of(me * slots, 8), slots)
     score_in[mine_at, :] = score[mine_at, :]
 
+    def drain_sum(s, _):
+        for d, u in every:
+            for copy in ring_copy(d, u, s):
+                copy.wait_send()
+        return 0
+
+    def drain_one():
+        def drain(i, _):
+            for p in range(ONE_CUTS):
+                one_copy(i, p).wait_send()
+            return 0
+
+        lax.fori_loop(1, experts, drain, 0)
+
+    def drain_two():
+        def drain(i, _):
+            for p in range(TWO_CUTS):
+                two_copy(i, p).wait_send()
+            return 0
+
+        lax.fori_loop(1, experts, drain, 0)
+
+    def drain_gather():
+        def drain_pass(r, _):
+            pass_copy(r, c).wait_send()
+            return 0
+
+        lax.fori_loop(0, half, drain_pass, 0)
+        lax.fori_loop(half + 1, n, drain_pass, 0)
+
+        def drain_down(s, _):
+            for d, u in every:
+                down_copy(d, u, s).wait_send()
+            return 0
+
+        lax.fori_loop(1, half - 1, drain_down, 0)
+        for d in range(2):
+            for h in range(2):
+                raw_copy(d, h).wait_send()
+        for u in range(2):
+            down_copy(u, u, half - 1).wait_send()
+            twin_copy(u).wait_send()
+
+    def land_score():
+        def land(i, _):
+            score_copy(i).wait()
+            return 0
+
+        lax.fori_loop(1, experts, land, 0)
+        for i in range(3):
+            head_copy(i).wait()
+
+    chores = (drain_one, drain_two, drain_gather, land_score)
+
     def body(s, _):
         k = half - s
         sib_copy(k).wait_recv()
@@ -532,9 +588,20 @@
         produce([k - 2, n - k + 2])
         sib_copy(k - 2).start()
         sib_copy(n - k + 2).start()
+
+        @pl.when(s > 1)
+        def _():
+            drain_sum(s - 1, 0)
+
+        for i, chore in enumerate(chores):
+            if i + 1 < half - 2:
+                pl.when(s == i + 1)(chore)
         return 0
 
     lax.fori_loop(1, half - 2, body, 0)
+    for i, chore in enumerate(chores):
+        if i + 1 >= half - 2:
+            chore()
     for s in range(max(1, half - 2), half):
         k = half - s
         sib_copy(k).wait_recv()
@@ -543,55 +610,14 @@
         if k == 2:
             prepare(half)
 
-    def land_score(i, _):
-        score_copy(i).wait()
-        return 0
-
-    lax.fori_loop(1, experts, land_score, 0)
+    heads_ref[...] = heads_in[...]
     router_ref[...] = jnp.sum(chosen * score_in[...], axis=0, keepdims=True)
-
-    def drain_one(i, _):
-        for p in range(ONE_CUTS):
-            one_copy(i, p).wait_send()
-        for p in range(TWO_CUTS):
-            two_copy(i, p).wait_send()
-        return 0
-
-    lax.fori_loop(1, experts, drain_one, 0)
-    for i in range(3):
-        head_copy(i).wait()
-    heads_ref[...] = heads_in[...]
-
-    def drain_pass(r, _):
-        pass_copy(r, c).wait_send()
-        return 0
-
-    lax.fori_loop(0, half, drain_pass, 0)
-    lax.fori_loop(half + 1, n, drain_pass, 0)
-
-    def drain_down(s, _):
-        for d, u in every:
-            down_copy(d, u, s).wait_send()
-        return 0
-
-    lax.fori_loop(1, half - 1, drain_down, 0)
-    for d in range(2):
-        for h in range(2):
-            raw_copy(d, h).wait_send()
-    for u in range(2):
-        down_copy(u, u, half - 1).wait_send()
-        twin_copy(u).wait_send()
-
-    def drain_sum(s, _):
-        for d, u in every:
-            for copy in ring_copy(d, u, s):
-                copy.wait_send()
-        return 0
 
     for d, u in every[:2]:
         for copy in ring_copy(d, u, 0):
             copy.wait_send()
-    lax.fori_loop(1, half - 1, drain_sum, 0)
+    for s in range(max(1, half - 3), half - 1):
+        drain_sum(s, 0)
     sib_copy(0).wait_recv()
 
     def finish(at, pieces):

time: 108 us -> 107 us (level)
  no operation moved by 1% of the time
where the time goes in v7:
time: 107 us
  Pallas kernels  107 us (100%)
    pallas_call x1, Pallas kernels, weight_gradient(): pl.pallas_call(functools.partial(grad_kernel, n, experts), out_shape=(jax...  102 us
    pallas_call x1, Pallas kernels, bucket_step(): pl.pallas_call(step_kernel, out_shape=[jax.ShapeDtypeStruct(master.shape,...  4.67 us

profile of v7, /device:TPU:1, one launch (start us, length us, event | category | flops | bytes accessed | tf_op | source)
XLA Modules:
  0.0 107.2 jit_solution(12620880637289754439)
XLA Ops:
  0.6 101.9 %shard_map.137 = (f32[80,1536]{1,0:T(8,128)}, f32[8,1536]{1,0:T(8,128)}, f32[1,128]{1,0:T(1,128)}, f32[3,1,3840]{2,1,0:T(1,128)}) custom-call(bf16[128,2560]{1,0:T(8,128)(2,1)} %tok_ref.1, bf16[128,2560]{1,0:T(8,128)(2,1)} %grad_ref.1, bf16[128,1536]{1,0:T(8,128)(2,1)} %bitcast.6, bf16[1,128]{1,0:T(2,128)(2,1)} %bitcast.9, s32[1,128]{1,0:T(1,128)} %bitcast.10, ...), custom_call_target="tpu_custom_call" | custom-call | flops 3296722944 | bytes 1081344 | tf_op jit(solution)/shard_map/pallas_call | solution.py:664
  102.5 4.7 %shard_map.138 = (f32[1,1,126720]{2,1,0:T(1,128)}, f32[1,1,126720]{2,1,0:T(1,128)}, f32[1,1,126720]{2,1,0:T(1,128)}, bf16[80,1536]{1,0:T(8,128)(2,1)}, f32[1,128]{1,0:T(1,128)}) custom-call(s32[33]{0:T(128)} %offset_ref.1, f32[80,1536]{1,0:T(8,128)} %get-tuple-element.14.block_ref, f32[8,1536]{1,0:T(8,128)} %get-tuple-element.15.below_ref, ...), custom_call_target="tpu_custom_call" | custom-call | tf_op jit(solution)/shard_map/pallas_call | solution.py:890
